TPU v7x, 128 devices: a whole 4x4x4 slice. The times are simulated.
128 devices in a mesh: row: 16 (over x, z_hi, core), col: 8 (over z_lo, y).
Axes of the slice: x: 4, y: 4, z: 4 (z_hi: 2, z_lo: 2; z = z_hi * 2 + z_lo), core: 2. Of those that a mesh axis runs over, the one named last changes fastest.
Arguments:
- homolog_embedding: bfloat16 [128, 1024, 256], P(None, ('row', 'col')), may hold values from -6 to 6
- standardizer_multiplier: float32 [256], replicated, may hold values from 0.5 to 1.5
- first_factor_matrix: bfloat16 [256, 32], replicated, may hold values from -0.375 to 0.375
- second_factor_matrix: bfloat16 [256, 32], replicated, may hold values from -0.375 to 0.375
- output_weight: bfloat16 [1024, 128], replicated, may hold values from -2.09375 to 2.09375
- cotangent: bfloat16 [1024, 16, 64, 128], P('row', None, 'col'), may hold values from -6 to 6
Outputs:
- pair_update_tiles: bfloat16 [1024, 16, 64, 128], P('row', None, 'col')
- alignment_gradient: bfloat16 [128, 1024, 256], P(None, ('row', 'col'))
- left_weight_gradient: float32 [256, 32], replicated
- right_weight_gradient: float32 [256, 32], replicated
- output_weight_gradient: float32 [1024, 128], replicated
- norm_gain_gradient: float32 [256], replicated
All inputs are finite; a program needn't handle non-finite values.
Results may differ from a plain program's by a relative error of at most 0.0079.
Values may be sent and summed in bfloat16 or wider, within the bound.
A program may use at most 128 MiB of HBM per device.

v0:
```python
import math

import jax
import jax.numpy as jnp
from jax import lax
from jax.sharding import PartitionSpec as P


def apply_layer_norm(values, standardizer_multiplier):
    inputs = values.astype(jnp.float32)
    center = inputs - jnp.mean(inputs, axis=-1, keepdims=True)
    inverse_deviation = lax.rsqrt(jnp.mean(center * center, axis=-1, keepdims=True) + 1e-05)
    scaled = center * inverse_deviation
    return (scaled, inverse_deviation, (scaled * standardizer_multiplier).astype(jnp.bfloat16))


def project(standardized_embedding, weight):
    return jnp.einsum(
        "sim,mc->ics", standardized_embedding, weight, preferred_element_type=jnp.float32
    ).astype(jnp.bfloat16)


def outer_tile(left_block, right_part):
    return jnp.einsum(
        "ics,jes->ijce", left_block, right_part, preferred_element_type=jnp.float32
    ).astype(jnp.bfloat16)


def outer_grad(cot_block, output_weight, sequence_total, width_ch):
    flat = cot_block.reshape(-1, cot_block.shape[-1])
    result = (
        jnp.dot(flat, output_weight.T, preferred_element_type=jnp.float32) / sequence_total
    ).astype(jnp.bfloat16)
    return result.reshape(cot_block.shape[0], cot_block.shape[1], width_ch, width_ch)


def on_device(
    homolog_embedding,
    standardizer_multiplier,
    first_factor_matrix,
    second_factor_matrix,
    output_weight,
    cotangent,
):
    centered_scaled, inverse_deviation, standardized_embedding = apply_layer_norm(
        homolog_embedding, standardizer_multiplier
    )
    left_local = project(standardized_embedding, first_factor_matrix)
    right_local = project(standardized_embedding, second_factor_matrix)
    sequence_total = homolog_embedding.shape[0]
    width_ch = first_factor_matrix.shape[1]
    width_cc = output_weight.shape[0]
    width_cz = output_weight.shape[1]
    left_rows = lax.all_gather(left_local, "col", axis=0, tiled=True)
    rows_i = left_rows.shape[0]
    block_rows = math.gcd(rows_i, 8)
    nblocks = rows_i // block_rows
    cot_flat = cotangent.reshape(rows_i, -1, width_cz)
    cols_j = cot_flat.shape[1]
    left_blocks = left_rows.reshape(nblocks, block_rows, width_ch, sequence_total)
    cot_blocks = cot_flat.reshape(nblocks, block_rows, cols_j, width_cz)

    def grads_from(left_block, cot_block, right_cols, grad_right):
        grad_outer = outer_grad(cot_block, output_weight, sequence_total, width_ch)
        left_part = jnp.einsum(
            "ijce,jes->ics", grad_outer, right_cols, preferred_element_type=jnp.float32
        )
        grad_right = grad_right + jnp.einsum(
            "ijce,ics->jes", grad_outer, left_block, preferred_element_type=jnp.float32
        )
        return (left_part, grad_right)

    zero_right = jnp.zeros((cols_j, width_ch, sequence_total), jnp.float32)
    zero_wout = jnp.zeros((width_cc, width_cz), jnp.float32)
    right_cols = lax.all_gather(right_local, "row", axis=0, tiled=True)

    def merged_block(carry, inputs):
        grad_wout, grad_right = carry
        left_block, cot_block = inputs
        outer_flat = outer_tile(left_block, right_cols).reshape(-1, width_cc)
        pair_blk = (
            jnp.dot(outer_flat, output_weight, preferred_element_type=jnp.float32) / sequence_total
        ).astype(jnp.bfloat16)
        grad_wout = grad_wout + jnp.dot(
            outer_flat.T, cot_block.reshape(-1, width_cz), preferred_element_type=jnp.float32
        )
        left_part, grad_right = grads_from(left_block, cot_block, right_cols, grad_right)
        return (
            (grad_wout, grad_right),
            (pair_blk.reshape(block_rows, cols_j, width_cz), left_part),
        )

    (grad_wout, grad_right), (pairs, left_parts) = lax.scan(
        merged_block, (zero_wout, zero_right), (left_blocks, cot_blocks)
    )
    pair_update_tiles = pairs.reshape(cotangent.shape)
    left_partial = left_parts.reshape(rows_i, width_ch, sequence_total)
    d_left = lax.psum_scatter(left_partial, "col", scatter_dimension=0, tiled=True).astype(
        jnp.bfloat16
    )
    d_right = lax.psum_scatter(grad_right, "row", scatter_dimension=0, tiled=True).astype(
        jnp.bfloat16
    )
    grad_wleft = jnp.einsum(
        "sim,ics->mc", standardized_embedding, d_left, preferred_element_type=jnp.float32
    )
    grad_wright = jnp.einsum(
        "sim,ics->mc", standardized_embedding, d_right, preferred_element_type=jnp.float32
    )
    standardized_cotangent = jnp.einsum(
        "ics,mc->sim", d_left, first_factor_matrix, preferred_element_type=jnp.float32
    )
    standardized_cotangent = standardized_cotangent + jnp.einsum(
        "ics,mc->sim", d_right, second_factor_matrix, preferred_element_type=jnp.float32
    )
    gain_gradient_sum = jnp.sum(standardized_cotangent * centered_scaled, axis=(0, 1))
    hidden_features = standardized_cotangent * standardizer_multiplier
    alignment_gradient = inverse_deviation * (
        hidden_features
        - jnp.mean(hidden_features, axis=-1, keepdims=True)
        - centered_scaled * jnp.mean(hidden_features * centered_scaled, axis=-1, keepdims=True)
    )
    running_totals = lax.psum(
        (grad_wout, grad_wleft, grad_wright, gain_gradient_sum), ("row", "col")
    )
    output_weight_gradient = running_totals[0] / sequence_total
    return (
        pair_update_tiles,
        alignment_gradient.astype(jnp.bfloat16),
        running_totals[1],
        running_totals[2],
        output_weight_gradient,
        running_totals[3],
    )


def solution(mesh):
    placed = (P(None, ("row", "col"), None), P(), P(), P(), P(), P("row", None, "col", None))
    return jax.shard_map(
        on_device,
        mesh=mesh,
        in_specs=placed,
        out_specs=(P("row", None, "col", None), P(None, ("row", "col"), None), P(), P(), P(), P()),
        check_vma=False,
    )
```

profile of v0, /device:TPU:1, one launch (start us, length us, event | category | flops | bytes accessed | tf_op | source)
XLA Modules:
  0.0 617.4 jit_solution(13006343109192623461)
XLA Ops:
  12.8 24.9 %all_gather.6 = bf16[64,32,128]{2,1,0:T(8,128)(2,1)S(1)} all-gather(bf16[8,32,128]{2,1,0:T(8,128)(2,1)S(1)} %fusion.28), channel_id=1, replica_groups=mesh['row'=16,'col'=8] {'col'}, dimensions={0}, use_global_device_ids=true | all-gather | bytes 589824 | tf_op jit(solution)/shard_map/all_gather | solution.py:54
  37.7 23.4 %all-gather.2.cloned.1.call-done = bf16[128,32,128]{2,1,0:T(8,128)(2,1)} async-done(((bf16[8,32,128]{2,1,0:T(8,128)(2,1)}), bf16[128,32,128]{2,1,0:T(8,128)(2,1)}) %all-gather.2.cloned.1.call-update) | async-done | bytes 1048592 | tf_op jit(solution)/shard_map/all_gather | solution.py:75
  62.7 141.9 %while.17 = (s32[]{:T(128)}, f32[1024,128]{1,0:T(8,128)}, f32[128,32,128]{2,0,1:T(8,128)}, bf16[8,8,128,128]{3,2,1,0:T(8,128)(2,1)}, f32[8,8,32,128]{3,2,1,0:T(8...) while((s32[]{:T(128)}, f32[1024,128]{1,0:T(8,128)}, ...), condition=%wide.region_3.4_spmd.clone, body=%wide.region_2.3_spmd.clone.sunk | while | flops 1615331328 | bytes 39715016 | solution.py:93
  69.5 2.6 copy.104
  72.1 2.2 copy.105
  75.1 2.4 bitcast_add_fusion.2
  82.7 2.6 fusion.83
  86.0 2.6 copy.104
  88.6 2.2 copy.105
  91.5 4.0 bitcast_add_fusion.2
  100.8 2.6 fusion.83
  104.0 2.6 copy.104
  109.6 4.0 bitcast_add_fusion.2
  118.8 2.6 fusion.83
  122.1 2.6 copy.104
  127.7 4.0 bitcast_add_fusion.2
  136.9 2.6 fusion.83
  140.2 2.6 copy.104
  145.7 4.0 bitcast_add_fusion.2
  155.0 2.6 fusion.83
  158.3 2.6 copy.104
  163.8 4.0 bitcast_add_fusion.2
  173.1 2.5 fusion.83
  176.3 2.6 copy.104
  181.9 4.0 bitcast_add_fusion.2
  191.1 2.6 fusion.83
  194.4 2.6 copy.104
  200.0 4.0 bitcast_add_fusion.2
  206.0 142.1 %all-reduce.4.cloned.1.call-done = f32[1024,128]{1,0:T(8,128)} async-done(((f32[1024,128]{1,0:T(8,128)}), f32[1024,128]{1,0:T(8,128)}) %all-reduce.4.cloned.1.call-update) | async-done | bytes 524304 | tf_op jit(solution)/shard_map/psum | solution.py:123
  350.0 33.5 %reduce-scatter.3.cloned.1.call-done = f32[8,32,128]{2,1,0:T(8,128)} async-done(((f32[64,32,128]{2,1,0:T(8,128)}), f32[8,32,128]{2,1,0:T(8,128)}) %reduce-scatter.3.cloned.1.call-update) | async-done | bytes 131088 | tf_op jit(solution)/shard_map/reduce_scatter | solution.py:98
  386.8 73.7 %reduce-scatter.5.cloned.1.call-done = f32[8,32,128]{2,0,1:T(8,128)} async-done(((f32[128,32,128]{2,0,1:T(8,128)}), f32[8,32,128]{2,0,1:T(8,128)}) %reduce-scatter.5.cloned.1.call-update) | async-done | bytes 131088 | tf_op jit(solution)/shard_map/reduce_scatter | solution.py:101
  465.8 141.1 %all-reduce.6.cloned.1.call-done = (f32[256,32]{0,1:T(8,128)}, f32[256,32]{0,1:T(8,128)}, f32[256]{0:T(256)}) async-done(((f32[256,32]{0,1:T(8,128)}, f32[256,32]{0,1:T(8,128)}, f32[256]{0:T(256)}), (f32[256,32]{0,1:T(8,128)}, f32[256,32]{0,1:T(8,128)}, f32[256]{0:T(256)})) %all-reduce.6.cloned.1.call-update) | async-done | bytes 66576 | tf_op jit(solution)/shard_map/psum | solution.py:123
  (148 shorter events, 90.8 us)
Async XLA Ops:
  7.2 2.8 copy-start
  7.2 5.1 copy-start.1
  7.2 5.1 copy-start.7
  7.2 5.1 copy-start.6
  7.2 53.8 %all-gather.2.cloned.1.call-start = ((), (), s32[]{:S(2)}) async-start(), calls=%async_computation.2 | async-start | bytes 1114112 | tf_op jit(solution)/shard_map/all_gather | solution.py:75
  12.2 50.5 %copy-start.3 = (bf16[1024,128]{1,0:T(8,128)(2,1)S(1)}, bf16[1024,128]{1,0:T(8,128)(2,1)}, u32[]{:S(2)}) copy-start(bf16[1024,128]{1,0:T(8,128)(2,1)} %param.12) | copy-start | bytes 786436
  12.2 336.0 %all-reduce.4.cloned.1.call-start = ((), (), s32[]{:S(2)}) async-start(), calls=%async_computation.5 | async-start | bytes 1048576 | tf_op jit(solution)/shard_map/psum | solution.py:123
  62.7 2.1 copy-start.4
  75.1 3.0 copy-start.5
  78.1 2.1 copy-start.4
  91.5 4.7 copy-start.5
  96.2 2.1 copy-start.4
  109.6 4.7 copy-start.5
  114.3 2.1 copy-start.4
  127.6 4.7 copy-start.5
  132.3 2.1 copy-start.4
  145.7 4.7 copy-start.5
  150.4 2.1 copy-start.4
  163.8 4.7 copy-start.5
  168.5 2.1 copy-start.4
  181.9 4.7 copy-start.5
  186.6 2.1 copy-start.4
  199.9 4.7 copy-start.5
  204.7 178.9 %reduce-scatter.3.cloned.1.call-start = ((), (), s32[]{:S(2)}) async-start(), calls=%async_computation.3 | async-start | bytes 1179648 | tf_op jit(solution)/shard_map/reduce_scatter | solution.py:98
  204.7 178.9 %copy-start.2 = (bf16[128,8,256]{2,1,0:T(8,128)(2,1)S(1)}, bf16[128,8,256]{2,1,0:T(8,128)(2,1)}, u32[]{:S(2)}) copy-start(bf16[128,8,256]{2,1,0:T(8,128)(2,1)} %param.8) | copy-start | bytes 1572868
  205.4 255.1 %reduce-scatter.5.cloned.1.call-start = ((), (), s32[]{:S(2)}) async-start(), calls=%async_computation.4 | async-start | bytes 2228224 | tf_op jit(solution)/shard_map/reduce_scatter | solution.py:101
  206.0 400.9 %all-reduce.6.cloned.1.call-start = ((), (), s32[]{:S(2)}) async-start(), calls=%async_computation.6 | async-start | bytes 133120 | tf_op jit(solution)/shard_map/psum | solution.py:123
Sparse Core Ops, SparseCore 0:
  12.3 48.6 all-gather.1
  204.8 143.3 all-reduce.3
  350.7 32.8 reduce-scatter.2
  387.9 72.5 reduce-scatter.4
  467.1 139.7 all-reduce.5
where the time goes:
time: 619 us; the launch traced here: 617 us
  waiting for transfers between devices  415 us (67%)
  matrix products  81.4 us (13%)
  local copies, waits for them, and re-layouts  75.1 us (12%)
  blocking collectives  24.9 us (4%)
  between operations  13.9 us (2%)
  other arithmetic  6.26 us (1%)
    psum x2, waiting for transfers between devices, on_device(): lax.psum((grad_wout, grad_wleft, grad_wright, gain_gradient_sum), ('row',...  283 us
    reduce_scatter x1, waiting for transfers between devices, on_device(): lax.psum_scatter(grad_right, 'row', scatter_dimension=0, tiled=True)  73.7 us
    reduce_scatter x1, waiting for transfers between devices, on_device(): lax.psum_scatter(left_partial, 'col', scatter_dimension=0, tiled=True)  33.5 us
    dot_general x8, matrix products, grads_from(): jnp.einsum('ijce,ics->jes', grad_outer, left_block, preferred_element_typ...  30.3 us
    all_gather x1, blocking collectives, on_device(): left_rows = lax.all_gather(left_local, 'col', axis=0, tiled=True)  24.9 us
    all_gather x1, waiting for transfers between devices, on_device(): right_cols = lax.all_gather(right_local, 'row', axis=0, tiled=True)  23.4 us
    convert_element_type x8, local copies, waits for them, and re-layouts, outer_grad(): result = (jnp.dot(flat, output_weight.T, preferred_element_type=jnp.float...  20.7 us
    dot_general x8, matrix products, merged_block(): jnp.dot(outer_flat.T, cot_block.reshape(-1, width_cz), preferred_element_...  19.4 us
  transfers between devices with their start and end apart: 5, of which 5 were waited for; matrix products, arithmetic and copies ran while one was open for 1% of the time, Pallas kernels for 0%

commit v1 on v0

v1 whole, which is shorter than its diff:
```python
import functools

import jax
import jax.numpy as jnp
from jax import lax
from jax.experimental import pallas as pl
from jax.experimental.pallas import tpu as pltpu
from jax.sharding import PartitionSpec as P

MESH = pl.DeviceIdType.MESH
BF = jnp.bfloat16
F32 = jnp.float32
NT = (((1,), (1,)), ((), ()))
TN = (((0,), (0,)), ((), ()))


def mm(a, b):
    return jnp.dot(a, b, preferred_element_type=F32)


def mm_nt(a, b):
    return lax.dot_general(a, b, NT, preferred_element_type=F32)


def mm_tn(a, b):
    return lax.dot_general(a, b, TN, preferred_element_type=F32)


def remote(src, dst, send_sem, recv_sem, **where):
    return pltpu.make_async_remote_copy(
        src_ref=src, dst_ref=dst, send_sem=send_sem, recv_sem=recv_sem,
        device_id=where, device_id_type=MESH,
    )


def aligned(start, size, multiple):
    return pl.ds(pl.multiple_of(start, multiple), size)


def kernel(
    n_row, n_col,
    x_ref, gamma_ref, w1_ref, w2_ref, wo_ref, g_hbm,
    z_hbm, ag_ref, wl_ref, wr_ref, dwo_ref, gain_ref,
    g_ref, xs, xh, nm, rs, wp, wpt, wf, rf, right_in, right, left, left_t, buf,
    dl_out, dl_in, dr_out, dr_sib, dr_in, dl_own, dr_own,
    dw_acc, dw_out, dw_in, dw_blk, dw_col, dw_full,
    sm_out, sm_in, sm_blk, sm_col, sm_full, z_buf,
    g_sem, z_sem,
    rg_s, rg_r, lg_s, lg_r, dl_s, dl_r, sib_s, sib_r, dr_s, dr_r,
    w1_s, w1_r, w2_s, w2_r, w3_s, w3_r, s1_s, s1_r, s2_s, s2_r, s3_s, s3_r,
):
    S, T, M = x_ref.shape
    C = w1_ref.shape[0]
    CC, K = wo_ref.shape
    J = n_row * T
    I = n_col * T
    B = T * C
    n_chip = n_row // 2
    inv = 1.0 / S
    row = lax.axis_index("row")
    col = lax.axis_index("col")
    chip = row // 2
    core = lax.rem(row, 2)
    sib = chip * 2 + 1 - core
    pending = []

    def send(c):
        c.start()
        pending.append(c)

    def other_row(d):
        return lax.rem(row + d, n_row)

    def other_col(d):
        return lax.rem(col + d, n_col)

    def other_chip(d):
        return lax.rem(chip + d, n_chip)

    barrier = pltpu.get_barrier_semaphore()
    for d in range(1, n_row):
        pl.semaphore_signal(barrier, inc=1, device_id={"row": other_row(d)}, device_id_type=MESH)
    for d in range(1, n_col):
        pl.semaphore_signal(barrier, inc=1, device_id={"col": other_col(d)}, device_id_type=MESH)

    g_copy = pltpu.make_async_copy(g_hbm, g_ref, g_sem)
    g_copy.start()

    wcat = jnp.concatenate([w1_ref[...], w2_ref[...]], axis=0)
    gamma = gamma_ref[...]
    wide = M // K
    x_all = x_ref[...].astype(F32).reshape(S * T, M)
    for a in range(wide):
        xs[a] = x_all[:, a * K:(a + 1) * K]
    for t in range(T):
        xt = jnp.concatenate([xs[a, pl.ds(t, S, stride=T), :] for a in range(wide)], axis=1)
        center = xt - jnp.mean(xt, axis=1, keepdims=True)
        rstd = lax.rsqrt(jnp.mean(center * center, axis=1, keepdims=True) + 1e-05)
        xhat = center * rstd
        normed = (xhat * gamma).astype(BF)
        xh[t] = xhat
        nm[t] = normed
        rs[t] = jnp.broadcast_to(rstd, (S, K))
        proj = mm_nt(wcat, normed)
        left[aligned(col * B + t * C, C, C), :] = proj[:C].astype(BF)
        rf[pl.ds(t, C, stride=T), :] = proj[C:]
    right_in[row] = rf[...].astype(BF)

    pl.semaphore_wait(barrier, n_row + n_col - 2)

    send(remote(right_in.at[row], right_in.at[row], rg_s.at[0], rg_r.at[row], row=sib))
    for d in range(1, n_chip):
        peer = other_chip(d) * 2 + core
        send(remote(right_in.at[row], right_in.at[row], rg_s.at[d], rg_r.at[row], row=peer))
    mine = aligned(col * B, B, B)
    for d in range(1, n_col):
        send(remote(left.at[mine], left.at[mine], lg_s.at[d], lg_r.at[col], col=other_col(d)))

    wf[...] = wo_ref[...].astype(F32)
    for e in range(C):
        wp[e * C:(e + 1) * C, :] = wf[pl.ds(e, C, stride=C), :].astype(BF)
    wpt[...] = wp[...].astype(F32).T.astype(BF)

    g_copy.wait()
    def go_step(p, _):
        res = mm_nt(wp[...], g_ref[aligned(p * 2 * J, 2 * J, 2 * J), :]).astype(BF)
        for a in range(2):
            for e in range(C):
                buf[aligned((2 * p + a) * C, C, C), e * J:(e + 1) * J] = (
                    res[e * C:(e + 1) * C, a * J:(a + 1) * J]
                )
        return 0
    lax.fori_loop(0, I // 2, go_step, 0)

    for d in range(1, n_chip):
        src = lax.rem(chip + n_chip - d, n_chip) * 2 + core
        remote(right_in.at[src], right_in.at[src], rg_s.at[d], rg_r.at[src], row=src).wait_recv()
        send(remote(right_in.at[src], right_in.at[src], rg_s.at[n_chip + d], rg_r.at[src], row=sib))
    remote(right_in.at[sib], right_in.at[sib], rg_s.at[0], rg_r.at[sib], row=sib).wait_recv()
    for d in range(1, n_chip):
        src = lax.rem(chip + n_chip - d, n_chip) * 2 + 1 - core
        remote(right_in.at[src], right_in.at[src], rg_s.at[0], rg_r.at[src], row=sib).wait_recv()

    def right_step(h, _):
        parts = [right_in[q, aligned(h * 2 * T, 2 * T, 2 * T), :].astype(F32) for q in range(n_row)]
        for a in range(2):
            tile = jnp.concatenate([p[a * T:(a + 1) * T] for p in parts], axis=0)
            right[aligned((2 * h + a) * J, J, J), :] = tile.astype(BF)
        return 0
    lax.fori_loop(0, C // 2, right_step, 0)

    def dl_step(k, _):
        owner = lax.rem(col + 1 + k, n_col)
        part = mm(buf[aligned(owner * B, B, B), :], right[...]) * inv
        dl_out[owner] = part.astype(BF)
        return 0
    for k in range(n_col):
        dl_step(k, 0)
        if k < n_col - 1:
            owner = other_col(k + 1)
            send(remote(dl_out.at[owner], dl_in.at[col], dl_s.at[k], dl_r.at[col], col=owner))

    for d in range(1, n_col):
        src = lax.rem(col + n_col - d, n_col)
        rows = aligned(src * B, B, B)
        remote(left.at[rows], left.at[rows], lg_s.at[d], lg_r.at[src], col=src).wait_recv()
    def turn_step(k, _):
        rows = aligned(k * B, B, B)
        left_t[k] = left[rows, :].astype(F32).T.astype(BF)
        return 0
    lax.fori_loop(0, n_col, turn_step, 0)

    def dr_step(h, _):
        lanes = aligned(h * 2 * J, 2 * J, 2 * J)
        acc = mm(left_t[0], buf[0:B, lanes])
        for k in range(1, n_col):
            acc = acc + mm(left_t[k], buf[k * B:(k + 1) * B, lanes])
        acc = acc * inv
        tiles = [acc[:, a * J:(a + 1) * J].T for a in range(2)]
        for q in range(n_row):
            blk = jnp.concatenate([t[q * T:(q + 1) * T] for t in tiles], axis=0)
            dr_out[q % 2, q // 2, aligned(h * 2 * T, 2 * T, 2 * T), :] = blk.astype(BF)
        return 0
    lax.fori_loop(0, C // 2, dr_step, 0)
    to_sib = remote(dr_out.at[1 - core], dr_sib, sib_s, sib_r, row=sib)
    send(to_sib)

    RB = 2 * B
    NB = 4 * J
    def outer_step(k, _):
        rows = aligned(k * RB, RB, RB)
        for n in range(C * J // NB):
            res = mm_nt(left[rows, :], right[n * NB:(n + 1) * NB, :])
            buf[rows, n * NB:(n + 1) * NB] = res.astype(BF)
        return 0
    lax.fori_loop(0, I * C // RB, outer_step, 0)

    to_sib.wait_recv()
    def pair_step(q, _):
        dr_sib[q] = (dr_out[core, q].astype(F32) + dr_sib[q].astype(F32)).astype(BF)
        return 0
    lax.fori_loop(0, n_chip, pair_step, 0)
    for d in range(1, n_chip):
        peer = other_chip(d)
        send(remote(dr_sib.at[peer], dr_in.at[chip], dr_s.at[d], dr_r.at[chip], row=peer * 2 + core))

    EH = C // 2
    RW = CC // n_row
    for h in range(2):
        dw_acc[...] = jnp.zeros_like(dw_acc)
        def dw_step(p, _):
            acc = None
            for b in range(2):
                lhs = jnp.concatenate([
                    jnp.concatenate([
                        buf[aligned((4 * p + 2 * b + a) * C, C, C), e * J:(e + 1) * J]
                        for e in range(h * EH, (h + 1) * EH)], axis=0)
                    for a in range(2)], axis=1)
                res = mm(lhs, g_ref[aligned((4 * p + 2 * b) * J, 2 * J, 2 * J), :])
                acc = res if acc is None else acc + res
            dw_acc[...] += acc
            return 0
        lax.fori_loop(0, I // 4, dw_step, 0)
        half = n_row // 2
        dw_out[h * half:(h + 1) * half] = dw_acc[...].astype(BF).reshape(half, RW, K)
    for d in range(1, n_row):
        peer = other_row(d)
        send(remote(dw_out.at[peer], dw_in.at[row], w1_s.at[d], w1_r.at[row], row=peer))

    dl_sum = dl_out[col].astype(F32)
    for d in range(1, n_col):
        src = lax.rem(col + n_col - d, n_col)
        remote(dl_in.at[src], dl_in.at[src], dl_s.at[0], dl_r.at[src], col=src).wait_recv()
        dl_sum = dl_sum + dl_in[src].astype(F32)
    dl_own[...] = dl_sum.astype(BF)
    dr_sum = dr_sib[chip].astype(F32)
    for d in range(1, n_chip):
        src = lax.rem(chip + n_chip - d, n_chip)
        remote(dr_in.at[src], dr_in.at[src], dr_s.at[d], dr_r.at[src], row=src * 2 + core).wait_recv()
        dr_sum = dr_sum + dr_in[src].astype(F32)
    dr_own[...] = dr_sum

    gain = jnp.zeros((1, M), F32)
    wgrad = jnp.zeros((2 * C, M), F32)
    for t in range(T):
        dcat = jnp.concatenate(
            [dl_own[t * C:(t + 1) * C, :], dr_own[pl.ds(t, C, stride=T), :].astype(BF)], axis=0)
        wgrad = wgrad + mm(dcat, nm[t])
        dn = mm_tn(dcat, wcat)
        xhat = xh[t]
        gain = gain + jnp.sum(dn * xhat, axis=0, keepdims=True)
        hid = dn * gamma
        m1 = jnp.mean(hid, axis=1, keepdims=True)
        m2 = jnp.mean(hid * xhat, axis=1, keepdims=True)
        rstd = rs[t]
        rstd = jnp.concatenate([rstd] * wide, axis=1)
        grad = rstd * (hid - m1 - xhat * m2)
        for a in range(wide):
            xs[a, pl.ds(t, S, stride=T), :] = grad[:, a * K:(a + 1) * K]
    grads = jnp.concatenate([xs[a] for a in range(wide)], axis=1)
    ag_ref[...] = grads.reshape(S, T, M).astype(BF)

    RS = 2 * C * wide // n_row
    gain_rows = jnp.concatenate([gain[:, a * K:(a + 1) * K] for a in range(wide)]
                                + [jnp.zeros((8 - wide, K), F32)], axis=0)
    for q in range(n_row):
        a, r0 = divmod(q * RS, 2 * C)
        sm_out[q, 0:RS, :] = wgrad[r0:r0 + RS, a * K:(a + 1) * K]
        sm_out[q, RS:RS + 8, :] = gain_rows
    for d in range(1, n_row):
        peer = other_row(d)
        send(remote(sm_out.at[peer], sm_in.at[row], s1_s.at[d], s1_r.at[row], row=peer))

    def sum_row(own, got, ss, rr):
        total = own.astype(F32)
        for d in range(1, n_row):
            src = lax.rem(row + n_row - d, n_row)
            remote(got.at[src], got.at[src], ss.at[d], rr.at[src], row=src).wait_recv()
            total = total + got[src].astype(F32)
        return total

    def sum_col(own, got, ss, rr):
        total = own
        for d in range(1, n_col):
            src = lax.rem(col + n_col - d, n_col)
            remote(got.at[src], got.at[src], ss.at[d], rr.at[src], col=src).wait_recv()
            total = total + got[src]
        return total

    def z_step(p, _):
        rhs = jnp.concatenate([
            jnp.concatenate([
                buf[aligned((2 * p + a) * C, C, C), e * J:(e + 1) * J] for e in range(C)], axis=0)
            for a in range(2)], axis=1)
        res = mm(wpt[...], rhs) * inv
        for a in range(2):
            z_buf[aligned((2 * p + a) * J, J, J), :] = res[:, a * J:(a + 1) * J].T.astype(BF)
        return 0

    z_copies = []
    def z_part(n, of):
        lo, hi = n * (I // 2) // of, (n + 1) * (I // 2) // of
        lax.fori_loop(lo, hi, z_step, 0)
        rows = pl.ds(lo * 2 * J, (hi - lo) * 2 * J)
        c = pltpu.make_async_copy(z_buf.at[rows], z_hbm.at[rows], z_sem.at[n])
        c.start()
        z_copies.append(c)

    dw_blk[0] = sum_row(dw_out[row], dw_in, w1_s, w1_r)
    for d in range(1, n_col):
        send(remote(dw_blk.at[0], dw_col.at[col], w2_s.at[d], w2_r.at[col], col=other_col(d)))
    z_part(0, 4)
    sm_blk[...] = sum_row(sm_out[row], sm_in, s1_s, s1_r)
    for d in range(1, n_col):
        send(remote(sm_blk, sm_col.at[col], s2_s.at[d], s2_r.at[col], col=other_col(d)))
    z_part(1, 4)
    dw_blk[1] = sum_col(dw_blk[0], dw_col, w2_s, w2_r) * inv
    dw_full[row] = dw_blk[1]
    for d in range(1, n_row):
        send(remote(dw_blk.at[1], dw_full.at[row], w3_s.at[d], w3_r.at[row], row=other_row(d)))
    z_part(2, 4)
    sm_full[row] = sum_col(sm_blk[...], sm_col, s2_s, s2_r)
    for d in range(1, n_row):
        send(remote(sm_full.at[row], sm_full.at[row], s3_s.at[d], s3_r.at[row], row=other_row(d)))
    z_part(3, 4)

    for d in range(1, n_row):
        src = lax.rem(row + n_row - d, n_row)
        remote(dw_full.at[src], dw_full.at[src], w3_s.at[d], w3_r.at[src], row=src).wait_recv()
    for e in range(C):
        q, r0 = divmod(e * C, RW)
        dwo_ref[pl.ds(e, C, stride=C), :] = dw_full[q, r0:r0 + C, :]
    for d in range(1, n_row):
        src = lax.rem(row + n_row - d, n_row)
        remote(sm_full.at[src], sm_full.at[src], s3_s.at[d], s3_r.at[src], row=src).wait_recv()
    for q in range(n_row):
        a, r0 = divmod(q * RS, 2 * C)
        for out, lo in ((wl_ref, 0), (wr_ref, C)):
            if lo <= r0 < lo + C:
                out[r0 - lo:r0 - lo + RS, a * K:(a + 1) * K] = sm_full[q, 0:RS, :]
    for a in range(wide):
        gain_ref[:, a * K:(a + 1) * K] = sm_full[0, RS + a:RS + a + 1, :]

    for c in z_copies:
        c.wait()
    for c in pending:
        c.wait_send()


def on_device(n_row, n_col, x, gamma, w1, w2, wo, cot):
    S, T, M = x.shape
    C = w1.shape[1]
    CC, K = wo.shape
    I, J = cot.shape[0], cot.shape[1] * cot.shape[2]
    B = T * C
    n_chip = n_row // 2
    RW = CC // n_row
    RS = 2 * C * (M // K) // n_row
    V = lambda shape, dtype: pltpu.VMEM(shape, dtype)
    D = lambda n: pltpu.SemaphoreType.DMA((n,))
    vm = pl.BlockSpec(memory_space=pltpu.VMEM)
    hb = pl.BlockSpec(memory_space=pl.ANY)
    z, ag, wl, wr, dwo, gain = pl.pallas_call(
        functools.partial(kernel, n_row, n_col),
        out_shape=(
            jax.ShapeDtypeStruct((I * J, K), BF),
            jax.ShapeDtypeStruct((S, T, M), BF),
            jax.ShapeDtypeStruct((C, M), F32),
            jax.ShapeDtypeStruct((C, M), F32),
            jax.ShapeDtypeStruct((CC, K), F32),
            jax.ShapeDtypeStruct((1, M), F32),
        ),
        in_specs=[vm, vm, vm, vm, vm, hb],
        out_specs=(hb, vm, vm, vm, vm, vm),
        scratch_shapes=[
            V((I * J, K), BF),
            V((M // K, S * T, K), F32),
            V((T, S, M), F32),
            V((T, S, M), BF),
            V((T, S, K), F32),
            V((CC, K), BF),
            V((K, CC), BF),
            V((CC, K), F32),
            V((B, S), F32),
            V((n_row, B, S), BF),
            V((C * J, S), BF),
            V((I * C, S), BF),
            V((n_col, S, B), BF),
            V((I * C, C * J), BF),
            V((n_col, B, S), BF),
            V((n_col, B, S), BF),
            V((2, n_chip, B, S), BF),
            V((n_chip, B, S), BF),
            V((n_chip, B, S), BF),
            V((B, S), BF),
            V((B, S), F32),
            V((CC // 2, K), F32),
            V((n_row, RW, K), BF),
            V((n_row, RW, K), BF),
            V((2, RW, K), F32),
            V((n_col, RW, K), F32),
            V((n_row, RW, K), F32),
            V((n_row, RS + 8, K), F32),
            V((n_row, RS + 8, K), F32),
            V((RS + 8, K), F32),
            V((n_col, RS + 8, K), F32),
            V((n_row, RS + 8, K), F32),
            V((I * J, K), BF),
            pltpu.SemaphoreType.DMA,
            D(4),
            D(n_row), D(n_row), D(n_col), D(n_col), D(n_col), D(n_col),
            pltpu.SemaphoreType.DMA, pltpu.SemaphoreType.DMA, D(n_chip), D(n_chip),
            D(n_row), D(n_row), D(n_col), D(n_col), D(n_row), D(n_row),
            D(n_row), D(n_row), D(n_col), D(n_col), D(n_row), D(n_row),
        ],
        compiler_params=pltpu.CompilerParams(
            collective_id=0, has_side_effects=True, vmem_limit_bytes=56 * 1024 * 1024,
        ),
    )(x, gamma.reshape(1, M), w1.T, w2.T, wo, cot.reshape(I * J, K))
    return z.reshape(cot.shape), ag, wl.T, wr.T, dwo, gain.reshape(M)


def solution(mesh):
    placed = (P(None, ("row", "col"), None), P(), P(), P(), P(), P("row", None, "col", None))
    return jax.shard_map(
        functools.partial(on_device, mesh.shape["row"], mesh.shape["col"]),
        mesh=mesh,
        in_specs=placed,
        out_specs=(P("row", None, "col", None), P(None, ("row", "col"), None), P(), P(), P(), P()),
        check_vma=False,
    )
```

time: 619 us -> 85.2 us (0.14)
  waiting for transfers between devices: 415 us -> 0 us
  matrix products: 81.4 us -> 0 us
  Pallas kernels: 0 us -> 77.7 us
  local copies, waits for them, and re-layouts: 75.1 us -> 6.64 us
  blocking collectives: 24.9 us -> 0 us
  between operations: 13.9 us -> 0.68 us
  other arithmetic: 6.26 us -> 0 us
    psum x2 -> x0, waiting for transfers between devices: 283 us -> none  [on_device(): lax.psum((grad_wout, grad_wleft, grad_wright, gain_gradient_sum), ('row',...]
    reduce_scatter x2 -> x0, waiting for transfers between devices: 107 us -> none  [the longest x1 73.7 us: on_device(): lax.psum_scatter(grad_right, 'row', scatter_dimension=0, tiled=True)]
    dot_general x54 -> x0, matrix products: 81.4 us -> none  [the longest x8 30.3 us: grads_from(): jnp.einsum('ijce,ics->jes', grad_outer, left_block, preferred_element_typ...]
    pallas_call x0 -> x1, Pallas kernels: none -> 77.7 us  [on_device(): pl.pallas_call(functools.partial(kernel, n_row, n_col), out_shape=(jax.Sh...]
    convert_element_type x16 -> x0, local copies, waits for them, and re-layouts: 31.6 us -> none  [the longest x8 20.7 us: outer_grad(): result = (jnp.dot(flat, output_weight.T, preferred_element_type=jnp.float...]
    all_gather x1 -> x0, blocking collectives: 24.9 us -> none  [on_device(): left_rows = lax.all_gather(left_local, 'col', axis=0, tiled=True)]
    all_gather x1 -> x0, waiting for transfers between devices: 23.4 us -> none  [on_device(): right_cols = lax.all_gather(right_local, 'row', axis=0, tiled=True)]
    dynamic_update_slice x16 -> x0, local copies, waits for them, and re-layouts: 19 us -> none  [on_device(): lax.scan(merged_block, (zero_wout, zero_right), (left_blocks, cot_blocks))]
  transfers between devices with their start and end apart: 5 -> 0, of which waited for: 5 -> 0; matrix products, arithmetic and copies ran while one was open for 1% -> 0% of each run, Pallas kernels for 0% -> 0%
where the time goes in v1:
time: 85.2 us; the launch traced here: 85 us
  Pallas kernels  77.7 us (91%)
  local copies, waits for them, and re-layouts  6.64 us (8%)
    pallas_call x1, Pallas kernels, on_device(): pl.pallas_call(functools.partial(kernel, n_row, n_col), out_shape=(jax.Sh...  77.7 us
    unnamed x16, local copies, waits for them, and re-layouts  6.64 us

profile of v1, /device:TPU:1, one launch (start us, length us, event | category | flops | bytes accessed | tf_op | source)
XLA Modules:
  0.0 85.0 jit_solution(7379431865927668084)
XLA Ops:
  0.6 77.7 %shard_map.109 = (bf16[8192,128]{1,0:T(8,128)(2,1)}, bf16[128,8,256]{2,1,0:T(8,128)(2,1)}, f32[32,256]{1,0:T(8,128)}, f32[32,256]{1,0:T(8,128)}, f32[1024,128]{1,0:T(8,128)}, /*index=5*/f32[1,256]{1,0:T(1,128)}) custom-call(bf16[128,8,256]{2,1,0:T(8,128)(2,1)} %x_ref.1, f32[1,256]{1,0:T(1,128)} %bitcast.14, bf16[32,256]{1,0:T(8,128)(2,1)} %bitcast.12, ...), custom_call_target="tpu_custom_call" | custom-call | tf_op jit(solution)/shard_map/pallas_call | solution.py:363
  78.4 0.0 copy-start.1
  78.4 0.0 copy-start.3
  78.4 0.0 copy-start.2
  78.4 0.0 copy-start
  78.4 3.2 %copy.18 = bf16[64,16,8,128]{3,2,1,0:T(8,128)(2,1)} copy(bf16[64,16,8,128]{3,2,1,0:T(8,128)(2,1)} %bitcast.9) | data formatting | bytes 4194304
  81.6 0.0 copy-done.1
  81.6 0.0 copy-start.4
  81.6 0.8 copy.19
  82.4 0.0 copy-done.3
  82.4 0.6 copy.20
  83.1 0.0 copy-done.2
  83.1 0.6 copy.21
  83.7 0.0 copy-done
  83.7 0.8 copy.22
  84.5 0.0 copy-done.4
  84.5 0.6 copy.23
Async XLA Ops:
  78.4 3.3 %copy-start.1 = (bf16[128,8,256]{2,1,0:T(8,128)(2,1)S(1)}, bf16[128,8,256]{2,1,0:T(8,128)(2,1)}, u32[]{:S(2)}) copy-start(bf16[128,8,256]{2,1,0:T(8,128)(2,1)} %get-tuple-element.25) | copy-start | bytes 1572868
  78.4 4.1 %copy-start.3 = (f32[32,256]{1,0:T(8,128)S(1)}, f32[32,256]{1,0:T(8,128)}, u32[]{:S(2)}) copy-start(f32[32,256]{1,0:T(8,128)} %get-tuple-element.14) | copy-start | bytes 98308
  78.4 4.7 %copy-start.2 = (f32[32,256]{1,0:T(8,128)S(1)}, f32[32,256]{1,0:T(8,128)}, u32[]{:S(2)}) copy-start(f32[32,256]{1,0:T(8,128)} %get-tuple-element.15) | copy-start | bytes 98308
  78.4 5.3 %copy-start = (f32[1024,128]{1,0:T(8,128)S(1)}, f32[1024,128]{1,0:T(8,128)}, u32[]{:S(2)}) copy-start(f32[1024,128]{1,0:T(8,128)} %get-tuple-element.28) | copy-start | bytes 1572868
  81.6 2.8 %copy-start.4 = (f32[1,256]{1,0:T(1,128)S(1)}, f32[1,256]{1,0:T(1,128)}, u32[]{:S(2)}) copy-start(f32[1,256]{1,0:T(1,128)} %get-tuple-element.17) | copy-start | bytes 3076

commit v2 on v1

--- a/solution.py
+++ b/solution.py
@@ -41,9 +41,9 @@
     n_row, n_col,
     x_ref, gamma_ref, w1_ref, w2_ref, wo_ref, g_hbm,
     z_hbm, ag_ref, wl_ref, wr_ref, dwo_ref, gain_ref,
-    g_ref, xs, xh, nm, rs, wp, wpt, wf, rf, right_in, right, left, left_t, buf,
+    g_ref, xs, xh, nm, rs, wp, wpt, wf, rf, right_in, right, left, left_t, g_out, buf,
     dl_out, dl_in, dr_out, dr_sib, dr_in, dl_own, dr_own,
-    dw_acc, dw_out, dw_in, dw_blk, dw_col, dw_full,
+    dw_out, dw_in, dw_blk, dw_col, dw_full,
     sm_out, sm_in, sm_blk, sm_col, sm_full, z_buf,
     g_sem, z_sem,
     rg_s, rg_r, lg_s, lg_r, dl_s, dl_r, sib_s, sib_r, dr_s, dr_r,
@@ -108,13 +108,13 @@
 
     pl.semaphore_wait(barrier, n_row + n_col - 2)
 
+    mine = aligned(col * B, B, B)
+    for d in range(1, n_col):
+        send(remote(left.at[mine], left.at[mine], lg_s.at[d], lg_r.at[col], col=other_col(d)))
     send(remote(right_in.at[row], right_in.at[row], rg_s.at[0], rg_r.at[row], row=sib))
     for d in range(1, n_chip):
         peer = other_chip(d) * 2 + core
         send(remote(right_in.at[row], right_in.at[row], rg_s.at[d], rg_r.at[row], row=peer))
-    mine = aligned(col * B, B, B)
-    for d in range(1, n_col):
-        send(remote(left.at[mine], left.at[mine], lg_s.at[d], lg_r.at[col], col=other_col(d)))
 
     wf[...] = wo_ref[...].astype(F32)
     for e in range(C):
@@ -122,15 +122,30 @@
     wpt[...] = wp[...].astype(F32).T.astype(BF)
 
     g_copy.wait()
-    def go_step(p, _):
-        res = mm_nt(wp[...], g_ref[aligned(p * 2 * J, 2 * J, 2 * J), :]).astype(BF)
-        for a in range(2):
-            for e in range(C):
-                buf[aligned((2 * p + a) * C, C, C), e * J:(e + 1) * J] = (
-                    res[e * C:(e + 1) * C, a * J:(a + 1) * J]
-                )
-        return 0
-    lax.fori_loop(0, I // 2, go_step, 0)
+    GN = 4 * J
+    for n in range(I * J // GN):
+        cols = slice(n * GN, (n + 1) * GN)
+        g_out[:, cols] = mm_nt(wp[...], g_ref[cols, :]).astype(BF)
+
+    for d in range(1, n_col):
+        src = lax.rem(col + n_col - d, n_col)
+        rows = aligned(src * B, B, B)
+        remote(left.at[rows], left.at[rows], lg_s.at[d], lg_r.at[src], col=src).wait_recv()
+    for k in range(I * C // S):
+        left_t[:, k * S:(k + 1) * S] = left[k * S:(k + 1) * S, :].T
+
+    for h in range(C // 2):
+        rhs = jnp.concatenate([
+            jnp.concatenate([
+                g_out[(2 * h + a) * C:(2 * h + a + 1) * C, i * J:(i + 1) * J] for a in range(2)], axis=1)
+            for i in range(I)], axis=0)
+        acc = mm(left_t[...], rhs) * inv
+        tiles = [acc[:, a * J:(a + 1) * J].T for a in range(2)]
+        for q in range(n_row):
+            blk = jnp.concatenate([t[q * T:(q + 1) * T] for t in tiles], axis=0)
+            dr_out[q % 2, q // 2, h * 2 * T:(h + 1) * 2 * T, :] = blk.astype(BF)
+    to_sib = remote(dr_out.at[1 - core], dr_sib, sib_s, sib_r, row=sib)
+    send(to_sib)
 
     for d in range(1, n_chip):
         src = lax.rem(chip + n_chip - d, n_chip) * 2 + core
@@ -149,52 +164,6 @@
         return 0
     lax.fori_loop(0, C // 2, right_step, 0)
 
-    def dl_step(k, _):
-        owner = lax.rem(col + 1 + k, n_col)
-        part = mm(buf[aligned(owner * B, B, B), :], right[...]) * inv
-        dl_out[owner] = part.astype(BF)
-        return 0
-    for k in range(n_col):
-        dl_step(k, 0)
-        if k < n_col - 1:
-            owner = other_col(k + 1)
-            send(remote(dl_out.at[owner], dl_in.at[col], dl_s.at[k], dl_r.at[col], col=owner))
-
-    for d in range(1, n_col):
-        src = lax.rem(col + n_col - d, n_col)
-        rows = aligned(src * B, B, B)
-        remote(left.at[rows], left.at[rows], lg_s.at[d], lg_r.at[src], col=src).wait_recv()
-    def turn_step(k, _):
-        rows = aligned(k * B, B, B)
-        left_t[k] = left[rows, :].astype(F32).T.astype(BF)
-        return 0
-    lax.fori_loop(0, n_col, turn_step, 0)
-
-    def dr_step(h, _):
-        lanes = aligned(h * 2 * J, 2 * J, 2 * J)
-        acc = mm(left_t[0], buf[0:B, lanes])
-        for k in range(1, n_col):
-            acc = acc + mm(left_t[k], buf[k * B:(k + 1) * B, lanes])
-        acc = acc * inv
-        tiles = [acc[:, a * J:(a + 1) * J].T for a in range(2)]
-        for q in range(n_row):
-            blk = jnp.concatenate([t[q * T:(q + 1) * T] for t in tiles], axis=0)
-            dr_out[q % 2, q // 2, aligned(h * 2 * T, 2 * T, 2 * T), :] = blk.astype(BF)
-        return 0
-    lax.fori_loop(0, C // 2, dr_step, 0)
-    to_sib = remote(dr_out.at[1 - core], dr_sib, sib_s, sib_r, row=sib)
-    send(to_sib)
-
-    RB = 2 * B
-    NB = 4 * J
-    def outer_step(k, _):
-        rows = aligned(k * RB, RB, RB)
-        for n in range(C * J // NB):
-            res = mm_nt(left[rows, :], right[n * NB:(n + 1) * NB, :])
-            buf[rows, n * NB:(n + 1) * NB] = res.astype(BF)
-        return 0
-    lax.fori_loop(0, I * C // RB, outer_step, 0)
-
     to_sib.wait_recv()
     def pair_step(q, _):
         dr_sib[q] = (dr_out[core, q].astype(F32) + dr_sib[q].astype(F32)).astype(BF)
@@ -204,25 +173,33 @@
         peer = other_chip(d)
         send(remote(dr_sib.at[peer], dr_in.at[chip], dr_s.at[d], dr_r.at[chip], row=peer * 2 + core))
 
-    EH = C // 2
+    for k in range(n_col):
+        owner = other_col(k + 1) if k < n_col - 1 else col
+        lhs = jnp.concatenate([
+            jnp.concatenate([
+                g_out[e * C:(e + 1) * C, aligned((owner * T + t) * J, J, J)] for t in range(T)], axis=0)
+            for e in range(C)], axis=1)
+        dl_out[owner] = (mm(lhs, right[...]) * inv).astype(BF)
+        if k < n_col - 1:
+            send(remote(dl_out.at[owner], dl_in.at[col], dl_s.at[k], dl_r.at[col], col=owner))
+
+    RB = I * C // 2
+    NB = 4 * J
+    for k in range(2):
+        for n in range(C * J // NB):
+            res = mm_nt(left[k * RB:(k + 1) * RB, :], right[n * NB:(n + 1) * NB, :])
+            buf[k * RB:(k + 1) * RB, n * NB:(n + 1) * NB] = res.astype(BF)
+
     RW = CC // n_row
-    for h in range(2):
-        dw_acc[...] = jnp.zeros_like(dw_acc)
-        def dw_step(p, _):
-            acc = None
-            for b in range(2):
-                lhs = jnp.concatenate([
-                    jnp.concatenate([
-                        buf[aligned((4 * p + 2 * b + a) * C, C, C), e * J:(e + 1) * J]
-                        for e in range(h * EH, (h + 1) * EH)], axis=0)
-                    for a in range(2)], axis=1)
-                res = mm(lhs, g_ref[aligned((4 * p + 2 * b) * J, 2 * J, 2 * J), :])
-                acc = res if acc is None else acc + res
-            dw_acc[...] += acc
-            return 0
-        lax.fori_loop(0, I // 4, dw_step, 0)
-        half = n_row // 2
-        dw_out[h * half:(h + 1) * half] = dw_acc[...].astype(BF).reshape(half, RW, K)
+    DN = 4
+    for h in range(DN):
+        lhs = jnp.concatenate([
+            jnp.concatenate([
+                buf[i * C:(i + 1) * C, e * J:(e + 1) * J]
+                for e in range(h * C // DN, (h + 1) * C // DN)], axis=0)
+            for i in range(I)], axis=1)
+        per = n_row // DN
+        dw_out[h * per:(h + 1) * per] = mm(lhs, g_ref[...]).astype(BF).reshape(per, RW, K)
     for d in range(1, n_row):
         peer = other_row(d)
         send(remote(dw_out.at[peer], dw_in.at[row], w1_s.at[d], w1_r.at[row], row=peer))
@@ -287,20 +264,20 @@
             total = total + got[src]
         return total
 
-    def z_step(p, _):
+    def z_step(p):
         rhs = jnp.concatenate([
             jnp.concatenate([
-                buf[aligned((2 * p + a) * C, C, C), e * J:(e + 1) * J] for e in range(C)], axis=0)
+                buf[(2 * p + a) * C:(2 * p + a + 1) * C, e * J:(e + 1) * J] for e in range(C)], axis=0)
             for a in range(2)], axis=1)
         res = mm(wpt[...], rhs) * inv
         for a in range(2):
-            z_buf[aligned((2 * p + a) * J, J, J), :] = res[:, a * J:(a + 1) * J].T.astype(BF)
-        return 0
+            z_buf[(2 * p + a) * J:(2 * p + a + 1) * J, :] = res[:, a * J:(a + 1) * J].T.astype(BF)
 
     z_copies = []
     def z_part(n, of):
         lo, hi = n * (I // 2) // of, (n + 1) * (I // 2) // of
-        lax.fori_loop(lo, hi, z_step, 0)
+        for p in range(lo, hi):
+            z_step(p)
         rows = pl.ds(lo * 2 * J, (hi - lo) * 2 * J)
         c = pltpu.make_async_copy(z_buf.at[rows], z_hbm.at[rows], z_sem.at[n])
         c.start()
@@ -385,7 +362,8 @@
             V((n_row, B, S), BF),
             V((C * J, S), BF),
             V((I * C, S), BF),
-            V((n_col, S, B), BF),
+            V((S, I * C), BF),
+            V((CC, I * J), BF),
             V((I * C, C * J), BF),
             V((n_col, B, S), BF),
             V((n_col, B, S), BF),
@@ -394,7 +372,6 @@
             V((n_chip, B, S), BF),
             V((B, S), BF),
             V((B, S), F32),
-            V((CC // 2, K), F32),
             V((n_row, RW, K), BF),
             V((n_row, RW, K), BF),
             V((2, RW, K), F32),

time: 85.2 us -> 75 us (0.88)
  Pallas kernels: 77.7 us -> 67.6 us
    pallas_call x1, Pallas kernels: 77.7 us -> 67.6 us  [on_device(): pl.pallas_call(functools.partial(kernel, n_row, n_col), out_shape=(jax.Sh...]
where the time goes in v2:
time: 75 us; the launch traced here: 74.9 us
  Pallas kernels  67.6 us (90%)
  local copies, waits for them, and re-layouts  6.64 us (9%)
    pallas_call x1, Pallas kernels, on_device(): pl.pallas_call(functools.partial(kernel, n_row, n_col), out_shape=(jax.Sh...  67.6 us
    unnamed x16, local copies, waits for them, and re-layouts  6.64 us

profile of v2, /device:TPU:1, one launch (start us, length us, event | category | flops | bytes accessed | tf_op | source)
XLA Modules:
  0.0 74.9 jit_solution(8857244954218949185)
XLA Ops:
  0.6 67.6 %shard_map.109 = (bf16[8192,128]{1,0:T(8,128)(2,1)}, bf16[128,8,256]{2,1,0:T(8,128)(2,1)}, f32[32,256]{1,0:T(8,128)}, f32[32,256]{1,0:T(8,128)}, f32[1024,128]{1,0:T(8,128)}, /*index=5*/f32[1,256]{1,0:T(1,128)}) custom-call(bf16[128,8,256]{2,1,0:T(8,128)(2,1)} %x_ref.1, f32[1,256]{1,0:T(1,128)} %bitcast.14, bf16[32,256]{1,0:T(8,128)(2,1)} %bitcast.12, ...), custom_call_target="tpu_custom_call" | custom-call | tf_op jit(solution)/shard_map/pallas_call | solution.py:340
  68.2 0.0 copy-start.1
  68.2 0.0 copy-start.3
  68.2 0.0 copy-start.2
  68.2 0.0 copy-start
  68.2 3.2 %copy.18 = bf16[64,16,8,128]{3,2,1,0:T(8,128)(2,1)} copy(bf16[64,16,8,128]{3,2,1,0:T(8,128)(2,1)} %bitcast.9) | data formatting | bytes 4194304
  71.5 0.0 copy-done.1
  71.5 0.0 copy-start.4
  71.5 0.8 %copy.19 = bf16[128,8,256]{2,1,0:T(8,128)(2,1)} copy(bf16[128,8,256]{2,1,0:T(8,128)(2,1)S(1)} %copy-done.1) | data formatting | bytes 1048576
  72.3 0.0 copy-done.3
  72.3 0.6 copy.20
  72.9 0.0 copy-done.2
  72.9 0.6 copy.21
  73.5 0.0 copy-done
  73.5 0.8 %copy.22 = f32[1024,128]{1,0:T(8,128)} copy(f32[1024,128]{1,0:T(8,128)S(1)} %copy-done) | data formatting | bytes 1048576
  74.3 0.0 copy-done.4
  74.3 0.6 copy.23
Async XLA Ops:
  68.2 3.3 %copy-start.1 = (bf16[128,8,256]{2,1,0:T(8,128)(2,1)S(1)}, bf16[128,8,256]{2,1,0:T(8,128)(2,1)}, u32[]{:S(2)}) copy-start(bf16[128,8,256]{2,1,0:T(8,128)(2,1)} %get-tuple-element.25) | copy-start | bytes 1572868
  68.2 4.1 %copy-start.3 = (f32[32,256]{1,0:T(8,128)S(1)}, f32[32,256]{1,0:T(8,128)}, u32[]{:S(2)}) copy-start(f32[32,256]{1,0:T(8,128)} %get-tuple-element.14) | copy-start | bytes 98308
  68.2 4.7 %copy-start.2 = (f32[32,256]{1,0:T(8,128)S(1)}, f32[32,256]{1,0:T(8,128)}, u32[]{:S(2)}) copy-start(f32[32,256]{1,0:T(8,128)} %get-tuple-element.15) | copy-start | bytes 98308
  68.2 5.3 %copy-start = (f32[1024,128]{1,0:T(8,128)S(1)}, f32[1024,128]{1,0:T(8,128)}, u32[]{:S(2)}) copy-start(f32[1024,128]{1,0:T(8,128)} %get-tuple-element.28) | copy-start | bytes 1572868
  71.5 2.8 %copy-start.4 = (f32[1,256]{1,0:T(1,128)S(1)}, f32[1,256]{1,0:T(1,128)}, u32[]{:S(2)}) copy-start(f32[1,256]{1,0:T(1,128)} %get-tuple-element.17) | copy-start | bytes 3076

commit v3 on v2

v3 whole, which is shorter than its diff:
```python
import functools

import jax
import jax.numpy as jnp
from jax import lax
from jax.experimental import pallas as pl
from jax.experimental.pallas import tpu as pltpu
from jax.sharding import PartitionSpec as P

MESH = pl.DeviceIdType.MESH
BF = jnp.bfloat16
F32 = jnp.float32
NT = (((1,), (1,)), ((), ()))
TN = (((0,), (0,)), ((), ()))


def mm(a, b):
    return jnp.dot(a, b, preferred_element_type=F32)


def mm_nt(a, b):
    return lax.dot_general(a, b, NT, preferred_element_type=F32)


def mm_tn(a, b):
    return lax.dot_general(a, b, TN, preferred_element_type=F32)


def remote(src, dst, send_sem, recv_sem, **where):
    return pltpu.make_async_remote_copy(
        src_ref=src, dst_ref=dst, send_sem=send_sem, recv_sem=recv_sem,
        device_id=where, device_id_type=MESH,
    )


def aligned(start, size, multiple):
    return pl.ds(pl.multiple_of(start, multiple), size)


def kernel(
    n_row, n_col,
    x_ref, gamma_ref, w1_ref, w2_ref, wo_ref, g_hbm,
    z_hbm, ag_hbm, wl_ref, wr_ref, dwo_ref, gain_ref,
    g_ref, xs, xh, nm, rs, wp, wpt, wf, rf, right_in, right, left, left_t, g_out, buf,
    dl_out, dl_in, dr_out, dr_sib, dr_in, dl_own, dr_own,
    dw_give, dw_sib, dw_own, dw_pair, dw_in, dw_blk, dw_chip, dw_full,
    sm_give, sm_sib, sm_own, sm_col, sm_sum, sm_chip, sm_half, z_buf, ag_buf,
    g_sem, z_sem, ag_sem, rg_s, rg_r, lg_s, lg_r, dl_s, dl_r, dr_s, dr_r,
    d1_s, d1_r, d2_s, d2_r, d3_s, d3_r, d4_s, d4_r, d5_s, d5_r,
    s1_s, s1_r, s2_s, s2_r, s3_s, s3_r, s4_s, s4_r,
):
    S, T, M = x_ref.shape
    C = w1_ref.shape[0]
    CC, K = wo_ref.shape
    J = n_row * T
    I = n_col * T
    B = T * C
    n_chip = n_row // 2
    inv = 1.0 / S
    row = lax.axis_index("row")
    col = lax.axis_index("col")
    chip = row // 2
    core = lax.rem(row, 2)
    sib = chip * 2 + 1 - core
    n_x, n_y = n_row // 4, n_col // 2
    x, zh = row // 4, lax.rem(row, 4) // 2
    zl, y = col // n_y, lax.rem(col, n_y)

    def row_of(dx, far, other):
        z = 1 - zh if far else zh
        return lax.rem(x + dx, n_x) * 4 + z * 2 + (1 - core if other else core)

    def col_of(dy, far):
        return (1 - zl if far else zl) * n_y + lax.rem(y + dy, n_y)

    pending = []

    def send(c):
        c.start()
        pending.append(c)

    def other_col(d):
        return lax.rem(col + d, n_col)

    def other_chip(d):
        return lax.rem(chip + d, n_chip)

    barrier = pltpu.get_barrier_semaphore()
    pl.semaphore_signal(barrier, inc=1, device_id={"row": sib}, device_id_type=MESH)
    for d in range(1, n_chip):
        peer = other_chip(d) * 2 + core
        pl.semaphore_signal(barrier, inc=1, device_id={"row": peer}, device_id_type=MESH)
    for d in range(1, n_col):
        pl.semaphore_signal(barrier, inc=1, device_id={"col": other_col(d)}, device_id_type=MESH)

    g_copy = pltpu.make_async_copy(g_hbm, g_ref, g_sem)
    g_copy.start()

    wcat = jnp.concatenate([w1_ref[...], w2_ref[...]], axis=0)
    gamma = gamma_ref[...]
    wide = M // K
    x_all = x_ref[...].astype(F32).reshape(S * T, M)
    for a in range(wide):
        xs[a] = x_all[:, a * K:(a + 1) * K]
    for t in range(T):
        xt = jnp.concatenate([xs[a, pl.ds(t, S, stride=T), :] for a in range(wide)], axis=1)
        center = xt - jnp.mean(xt, axis=1, keepdims=True)
        rstd = lax.rsqrt(jnp.mean(center * center, axis=1, keepdims=True) + 1e-05)
        xhat = center * rstd
        normed = (xhat * gamma).astype(BF)
        xh[t] = xhat
        nm[t] = normed
        rs[t] = jnp.broadcast_to(rstd, (S, K))
        proj = mm_nt(wcat, normed)
        left[aligned(col * B + t * C, C, C), :] = proj[:C].astype(BF)
        rf[pl.ds(t, C, stride=T), :] = proj[C:]
    right_in[row] = rf[...].astype(BF)

    pl.semaphore_wait(barrier, n_chip + n_col - 1)

    def left_rows(c):
        return aligned(c * B, B, B)

    def send_right(block, slot, to):
        send(remote(right_in.at[block], right_in.at[block], rg_s.at[slot], rg_r.at[block], row=to))

    def wait_right(block):
        remote(right_in.at[block], right_in.at[block], rg_s.at[0], rg_r.at[block], row=sib).wait_recv()

    def send_left(block, slot, to):
        rows = left_rows(block)
        send(remote(left.at[rows], left.at[rows], lg_s.at[slot], lg_r.at[block], col=to))

    def wait_left(block):
        rows = left_rows(block)
        remote(left.at[rows], left.at[rows], lg_s.at[0], lg_r.at[block], col=col_of(0, True)).wait_recv()

    send_right(row, 0, row_of(0, True, False))
    send_left(col, 0, col_of(0, True))
    for d in range(1, n_x):
        send_right(row, d, row_of(d, False, False))
    for d in range(1, n_y):
        send_left(col, d, col_of(d, False))
    send_right(row, 2 * n_x, sib)

    wf[...] = wo_ref[...].astype(F32)
    for e in range(C):
        wp[e * C:(e + 1) * C, :] = wf[pl.ds(e, C, stride=C), :].astype(BF)
    wpt[...] = wp[...].astype(F32).T.astype(BF)

    g_copy.wait()
    GN = 4 * J

    def g_outer_part(lo, hi):
        for n in range(lo, hi):
            cols = slice(n * GN, (n + 1) * GN)
            g_out[:, cols] = mm_nt(wp[...], g_ref[cols, :]).astype(BF)

    n_go = I * J // GN
    g_outer_part(0, n_go // 2)

    far_row, far_col = row_of(0, True, False), col_of(0, True)
    wait_right(far_row)
    for d in range(1, n_x):
        send_right(far_row, n_x + d, row_of(d, False, False))
    send_right(far_row, n_x, sib)
    wait_left(far_col)
    for d in range(1, n_y):
        send_left(far_col, n_y + d, col_of(d, False))

    g_outer_part(n_go // 2, n_go)

    for d in range(1, n_x):
        block = row_of(d, False, False)
        wait_right(block)
        send_right(block, 2 * n_x + d, sib)
    for d in range(1, n_y):
        wait_left(col_of(d, False))
    for d in range(1, n_y):
        wait_left(col_of(d, True))
    for d in range(1, n_x):
        block = row_of(d, True, False)
        wait_right(block)
        send_right(block, 3 * n_x + d, sib)
    for k in range(I * C // S):
        left_t[:, k * S:(k + 1) * S] = left[k * S:(k + 1) * S, :].T

    for h in range(C // 2):
        rhs = jnp.concatenate([
            jnp.concatenate([
                g_out[(2 * h + a) * C:(2 * h + a + 1) * C, i * J:(i + 1) * J] for a in range(2)], axis=1)
            for i in range(I)], axis=0)
        acc = mm(left_t[...], rhs) * inv
        tiles = [acc[:, a * J:(a + 1) * J].T for a in range(2)]
        for q in range(n_row):
            blk = jnp.concatenate([t[q * T:(q + 1) * T] for t in tiles], axis=0)
            dr_out[q % 2, q // 2, h * 2 * T:(h + 1) * 2 * T, :] = blk.astype(BF)
    to_sib = remote(dr_out.at[1 - core], dr_sib, dr_s.at[0], dr_r.at[n_chip], row=sib)
    send(to_sib)

    for far in (False, True):
        for d in range(n_x):
            wait_right(row_of(d, far, True))
    def right_step(h, _):
        parts = [right_in[q, aligned(h * 2 * T, 2 * T, 2 * T), :].astype(F32) for q in range(n_row)]
        for a in range(2):
            tile = jnp.concatenate([p[a * T:(a + 1) * T] for p in parts], axis=0)
            right[aligned((2 * h + a) * J, J, J), :] = tile.astype(BF)
        return 0
    lax.fori_loop(0, C // 2, right_step, 0)

    def right_grad_out():
        to_sib.wait_recv()
        def pair_step(q, _):
            dr_sib[q] = (dr_out[core, q].astype(F32) + dr_sib[q].astype(F32)).astype(BF)
            return 0
        lax.fori_loop(0, n_chip, pair_step, 0)
        for d in range(1, n_chip):
            peer = other_chip(d)
            send(remote(dr_sib.at[peer], dr_in.at[chip], dr_s.at[d], dr_r.at[chip], row=peer * 2 + core))

    for k in range(n_col):
        owner = other_col(k + 1) if k < n_col - 1 else col
        lhs = jnp.concatenate([
            jnp.concatenate([
                g_out[e * C:(e + 1) * C, aligned((owner * T + t) * J, J, J)] for t in range(T)], axis=0)
            for e in range(C)], axis=1)
        dl_out[owner] = (mm(lhs, right[...]) * inv).astype(BF)
        if k == n_col // 2 - 1:
            right_grad_out()
        if k < n_col - 1:
            send(remote(dl_out.at[owner], dl_in.at[col], dl_s.at[k], dl_r.at[col], col=owner))

    RB = I * C // 2
    NB = 4 * J
    for k in range(2):
        for n in range(C * J // NB):
            res = mm_nt(left[k * RB:(k + 1) * RB, :], right[n * NB:(n + 1) * NB, :])
            buf[k * RB:(k + 1) * RB, n * NB:(n + 1) * NB] = res.astype(BF)

    HW = CC // 2
    QE = C // 4

    def dw_quarter(e0):
        lhs = jnp.concatenate([
            jnp.concatenate([
                buf[i * C:(i + 1) * C, aligned((e0 + e) * J, J, J)] for e in range(QE)], axis=0)
            for i in range(I)], axis=1)
        return mm(lhs, g_ref[...])

    for q in range(2):
        rows = slice(q * HW // 2, (q + 1) * HW // 2)
        dw_give[rows, :] = dw_quarter((1 - core) * 2 * QE + q * QE).astype(BF)
    dw_to_sib = remote(dw_give, dw_sib, d1_s, d1_r, row=sib)
    send(dw_to_sib)
    for q in range(2):
        rows = slice(q * HW // 2, (q + 1) * HW // 2)
        dw_own[rows, :] = dw_quarter(core * 2 * QE + q * QE)

    RW = HW // n_col
    dw_to_sib.wait_recv()
    dw_pair[...] = (dw_own[...] + dw_sib[...].astype(F32)).astype(BF).reshape(n_col, RW, K)
    for d in range(1, n_col):
        peer = other_col(d)
        send(remote(dw_pair.at[peer], dw_in.at[col], d2_s.at[d], d2_r.at[col], col=peer))

    dl_sum = dl_out[col].astype(F32)
    for d in range(1, n_col):
        src = lax.rem(col + n_col - d, n_col)
        remote(dl_in.at[src], dl_in.at[src], dl_s.at[0], dl_r.at[src], col=src).wait_recv()
        dl_sum = dl_sum + dl_in[src].astype(F32)
    dl_own[...] = dl_sum.astype(BF)
    dr_sum = dr_sib[chip].astype(F32)
    for d in range(1, n_chip):
        src = lax.rem(chip + n_chip - d, n_chip)
        remote(dr_in.at[src], dr_in.at[src], dr_s.at[d], dr_r.at[src], row=src * 2 + core).wait_recv()
        dr_sum = dr_sum + dr_in[src].astype(F32)
    dr_own[...] = dr_sum

    gain = jnp.zeros((1, M), F32)
    wgrad = jnp.zeros((2 * C, M), F32)
    for t in range(T):
        dcat = jnp.concatenate(
            [dl_own[t * C:(t + 1) * C, :], dr_own[pl.ds(t, C, stride=T), :].astype(BF)], axis=0)
        wgrad = wgrad + mm(dcat, nm[t])
        dn = mm_tn(dcat, wcat)
        xhat = xh[t]
        gain = gain + jnp.sum(dn * xhat, axis=0, keepdims=True)
        hid = dn * gamma
        m1 = jnp.mean(hid, axis=1, keepdims=True)
        m2 = jnp.mean(hid * xhat, axis=1, keepdims=True)
        rstd = rs[t]
        rstd = jnp.concatenate([rstd] * wide, axis=1)
        grad = rstd * (hid - m1 - xhat * m2)
        for a in range(wide):
            xs[a, pl.ds(t, S, stride=T), :] = grad[:, a * K:(a + 1) * K]
    grads = jnp.concatenate([xs[a] for a in range(wide)], axis=1)
    ag_buf[...] = grads.reshape(S, T, M).astype(BF)
    ag_copy = pltpu.make_async_copy(ag_buf, ag_hbm, ag_sem)
    ag_copy.start()

    RS = 2 * C
    for a in range(wide):
        sm_own[a, 0:RS, :] = wgrad[:, a * K:(a + 1) * K]
        sm_own[a, RS:RS + 8, :] = jnp.broadcast_to(gain[:, a * K:(a + 1) * K], (8, K))
    sm_to_sib = remote(sm_own.at[1 - core], sm_sib, s1_s, s1_r, row=sib)
    send(sm_to_sib)

    def sum_chips(own, got, ss, rr):
        total = own
        for d in range(1, n_chip):
            src = lax.rem(chip + n_chip - d, n_chip)
            remote(got.at[src], got.at[src], ss.at[d], rr.at[src], row=src * 2 + core).wait_recv()
            total = total + got[src].astype(F32)
        return total

    def sum_cols(own, got, ss, rr):
        total = own
        for d in range(1, n_col):
            src = lax.rem(col + n_col - d, n_col)
            remote(got.at[src], got.at[src], ss.at[d], rr.at[src], col=src).wait_recv()
            total = total + got[src].astype(F32)
        return total

    def to_chips(src, dst, ss, rr):
        for d in range(1, n_chip):
            peer = other_chip(d) * 2 + core
            send(remote(src, dst.at[chip], ss.at[d], rr.at[chip], row=peer))

    def to_cols(src, dst, ss, rr):
        for d in range(1, n_col):
            send(remote(src, dst.at[col], ss.at[d], rr.at[col], col=other_col(d)))

    def z_step(p):
        rhs = jnp.concatenate([
            jnp.concatenate([
                buf[(2 * p + a) * C:(2 * p + a + 1) * C, e * J:(e + 1) * J] for e in range(C)], axis=0)
            for a in range(2)], axis=1)
        res = mm(wpt[...], rhs) * inv
        for a in range(2):
            z_buf[(2 * p + a) * J:(2 * p + a + 1) * J, :] = res[:, a * J:(a + 1) * J].T.astype(BF)

    z_copies = []
    def z_part(n, of):
        lo, hi = n * (I // 2) // of, (n + 1) * (I // 2) // of
        for p in range(lo, hi):
            z_step(p)
        rows = pl.ds(lo * 2 * J, (hi - lo) * 2 * J)
        c = pltpu.make_async_copy(z_buf.at[rows], z_hbm.at[rows], z_sem.at[n])
        c.start()
        z_copies.append(c)

    z_part(0, 4)
    sm_to_sib.wait_recv()
    sm_give[...] = sm_own[core] + sm_sib[...]
    to_cols(sm_give, sm_col, s2_s, s2_r)
    z_part(1, 4)
    own = dw_pair[col].astype(F32)
    dw_blk[0] = sum_cols(own, dw_in, d2_s, d2_r).astype(BF)
    to_chips(dw_blk.at[0], dw_chip, d3_s, d3_r)
    z_part(2, 4)
    sm_sum[...] = sum_cols(sm_give[...], sm_col, s2_s, s2_r)
    to_chips(sm_sum, sm_chip, s3_s, s3_r)
    z_part(3, 4)
    dw_blk[1] = (sum_chips(dw_blk[0].astype(F32), dw_chip, d3_s, d3_r) * inv).astype(BF)
    to_cols(dw_blk.at[1], dw_full.at[core], d4_s, d4_r)
    dw_full[core, col] = dw_blk[1]
    sm_half[core] = sum_chips(sm_sum[...], sm_chip, s3_s, s3_r)
    sm_back = remote(sm_half.at[core], sm_half.at[core], s4_s, s4_r.at[core], row=sib)
    send(sm_back)
    for d in range(1, n_col):
        src = lax.rem(col + n_col - d, n_col)
        got = dw_full.at[core, src]
        remote(got, got, d4_s.at[d], d4_r.at[src], col=src).wait_recv()
    send(remote(dw_full.at[core], dw_full.at[core], d5_s, d5_r.at[core], row=sib))

    def put_dw(h):
        per = RW // C
        for e in range(C // 2):
            part = dw_full[h, e // per].astype(F32)
            dwo_ref[pl.ds(h * (C // 2) + e, C, stride=C), :] = part[(e % per) * C:(e % per + 1) * C]

    got = sm_half.at[1 - core]
    remote(got, got, s4_s, s4_r.at[1 - core], row=sib).wait_recv()
    for a in range(wide):
        lanes = slice(a * K, (a + 1) * K)
        wl_ref[:, lanes] = sm_half[a, 0:C, :]
        wr_ref[:, lanes] = sm_half[a, C:2 * C, :]
        gain_ref[:, lanes] = sm_half[a, RS:RS + 1, :]
    got = dw_full.at[1 - core]
    remote(got, got, d5_s, d5_r.at[1 - core], row=sib).wait_recv()
    put_dw(0)
    put_dw(1)

    ag_copy.wait()
    for c in z_copies:
        c.wait()
    for c in pending:
        c.wait_send()


def settle_kernel(*refs):
    n = (len(refs) - 2) // 3
    srcs, dsts, held = refs[:n], refs[n:2 * n], refs[2 * n:3 * n]
    in_sems, out_sems = refs[3 * n:]
    loads, stores = [], []
    for src, dst, mid in zip(srcs, dsts, held):
        parts = 4 if src.shape[0] >= 4096 else 1
        rows = src.shape[0] // parts
        for p in range(parts):
            part = pl.ds(p * rows, rows)
            k = len(loads)
            loads.append(pltpu.make_async_copy(src.at[part], mid.at[part], in_sems.at[k]))
            stores.append(pltpu.make_async_copy(mid.at[part], dst.at[part], out_sems.at[k]))
            loads[-1].start()
    for load, store in zip(loads, stores):
        load.wait()
        store.start()
    for store in stores:
        store.wait()


def settle(arrays):
    hb = pl.BlockSpec(memory_space=pl.ANY)
    sems = pltpu.SemaphoreType.DMA((len(arrays) + 3,))
    return pl.pallas_call(
        settle_kernel,
        out_shape=tuple(jax.ShapeDtypeStruct(a.shape, a.dtype) for a in arrays),
        in_specs=[hb] * len(arrays),
        out_specs=(hb,) * len(arrays),
        scratch_shapes=[pltpu.VMEM(a.shape, a.dtype) for a in arrays] + [sems, sems],
        compiler_params=pltpu.CompilerParams(vmem_limit_bytes=62 * 1024 * 1024),
    )(*arrays)


def on_device(n_row, n_col, x, gamma, w1, w2, wo, cot):
    S, T, M = x.shape
    C = w1.shape[1]
    CC, K = wo.shape
    I, J = cot.shape[0], cot.shape[1] * cot.shape[2]
    B = T * C
    n_chip = n_row // 2
    RW = CC // 2 // n_col
    RS = 2 * C + 8
    one = pltpu.SemaphoreType.DMA
    V = lambda shape, dtype: pltpu.VMEM(shape, dtype)
    D = lambda n: pltpu.SemaphoreType.DMA((n,))
    vm = pl.BlockSpec(memory_space=pltpu.VMEM)
    hb = pl.BlockSpec(memory_space=pl.ANY)
    z, ag, wl, wr, dwo, gain = pl.pallas_call(
        functools.partial(kernel, n_row, n_col),
        out_shape=(
            jax.ShapeDtypeStruct((I * J, K), BF),
            jax.ShapeDtypeStruct((S, T, M), BF),
            jax.ShapeDtypeStruct((C, M), F32),
            jax.ShapeDtypeStruct((C, M), F32),
            jax.ShapeDtypeStruct((CC, K), F32),
            jax.ShapeDtypeStruct((1, M), F32),
        ),
        in_specs=[vm, vm, vm, vm, vm, hb],
        out_specs=(hb, hb, vm, vm, vm, vm),
        scratch_shapes=[
            V((I * J, K), BF),
            V((M // K, S * T, K), F32),
            V((T, S, M), F32),
            V((T, S, M), BF),
            V((T, S, K), F32),
            V((CC, K), BF),
            V((K, CC), BF),
            V((CC, K), F32),
            V((B, S), F32),
            V((n_row, B, S), BF),
            V((C * J, S), BF),
            V((I * C, S), BF),
            V((S, I * C), BF),
            V((CC, I * J), BF),
            V((I * C, C * J), BF),
            V((n_col, B, S), BF),
            V((n_col, B, S), BF),
            V((2, n_chip, B, S), BF),
            V((n_chip, B, S), BF),
            V((n_chip, B, S), BF),
            V((B, S), BF),
            V((B, S), F32),
            V((CC // 2, K), BF),
            V((CC // 2, K), BF),
            V((CC // 2, K), F32),
            V((n_col, RW, K), BF),
            V((n_col, RW, K), BF),
            V((2, RW, K), BF),
            V((n_chip, RW, K), BF),
            V((2, n_col, RW, K), BF),
            V((RS, K), F32),
            V((RS, K), F32),
            V((2, RS, K), F32),
            V((n_col, RS, K), F32),
            V((RS, K), F32),
            V((n_chip, RS, K), F32),
            V((2, RS, K), F32),
            V((I * J, K), BF),
            V((S, T, M), BF),
            one, D(4), one,
            D(n_row), D(n_row), D(n_col), D(n_col), D(n_col), D(n_col), D(n_chip), D(n_chip + 1),
            one, one, D(n_col), D(n_col), D(n_chip), D(n_chip), D(n_col), D(n_col), one, D(2),
            one, one, D(n_col), D(n_col), D(n_chip), D(n_chip), one, D(2),
        ],
        compiler_params=pltpu.CompilerParams(
            collective_id=0, has_side_effects=True, vmem_limit_bytes=56 * 1024 * 1024,
        ),
    )(x, gamma.reshape(1, M), w1.T, w2.T, wo, cot.reshape(I * J, K))
    z, ag, wl, wr, dwo, gain = settle((z, ag, wl, wr, dwo, gain))
    return z.reshape(cot.shape), ag, wl.T, wr.T, dwo, gain.reshape(M)


def solution(mesh):
    placed = (P(None, ("row", "col"), None), P(), P(), P(), P(), P("row", None, "col", None))
    return jax.shard_map(
        functools.partial(on_device, mesh.shape["row"], mesh.shape["col"]),
        mesh=mesh,
        in_specs=placed,
        out_specs=(P("row", None, "col", None), P(None, ("row", "col"), None), P(), P(), P(), P()),
        check_vma=False,
    )
```

time: 75 us -> 62 us (0.83)
  local copies, waits for them, and re-layouts: 6.64 us -> 0 us
  Pallas kernels: 67.6 us -> 61 us
    pallas_call x1, Pallas kernels: 67.6 us -> 58.1 us  [on_device(): pl.pallas_call(functools.partial(kernel, n_row, n_col), out_shape=(jax.Sh...]
    unnamed x16 -> x0, local copies, waits for them, and re-layouts: 6.64 us -> none
    pallas_call x0 -> x1, Pallas kernels: none -> 2.88 us  [settle(): pl.pallas_call(settle_kernel, out_shape=tuple((jax.ShapeDtypeStruct(a.sha...]
where the time goes in v3:
time: 62 us; the launch traced here: 61.8 us
  Pallas kernels  61 us (98%)
  between operations  0.82 us (1%)
    pallas_call x1, Pallas kernels, on_device(): pl.pallas_call(functools.partial(kernel, n_row, n_col), out_shape=(jax.Sh...  58.1 us
    pallas_call x1, Pallas kernels, settle(): pl.pallas_call(settle_kernel, out_shape=tuple((jax.ShapeDtypeStruct(a.sha...  2.88 us

profile of v3, /device:TPU:1, one launch (start us, length us, event | category | flops | bytes accessed | tf_op | source)
XLA Modules:
  0.0 61.8 jit_solution(3810930647037888286)
XLA Ops:
  0.6 58.1 %shard_map.109 = (bf16[8192,128]{1,0:T(8,128)(2,1)}, bf16[128,8,256]{2,1,0:T(8,128)(2,1)}, f32[32,256]{1,0:T(8,128)}, f32[32,256]{1,0:T(8,128)}, f32[1024,128]{1,0:T(8,128)}, /*index=5*/f32[1,256]{1,0:T(1,128)}) custom-call(bf16[128,8,256]{2,1,0:T(8,128)(2,1)} %x_ref.1, f32[1,256]{1,0:T(1,128)} %bitcast.11, bf16[32,256]{1,0:T(8,128)(2,1)} %bitcast.9, ...), custom_call_target="tpu_custom_call" | custom-call | tf_op jit(solution)/shard_map/pallas_call | solution.py:450
  58.8 2.9 %shard_map.110 = (bf16[8192,128]{1,0:T(8,128)(2,1)}, bf16[128,8,256]{2,1,0:T(8,128)(2,1)}, f32[32,256]{1,0:T(8,128)}, f32[32,256]{1,0:T(8,128)}, f32[1024,128]{1,0:T(8,128)}, /*index=5*/f32[1,256]{1,0:T(1,128)}) custom-call(bf16[8192,128]{1,0:T(8,128)(2,1)} %get-tuple-element.18.refs_0_, bf16[128,8,256]{2,1,0:T(8,128)(2,1)} %get-tuple-element.19.refs_1_, ...), custom_call_target="tpu_custom_call" | custom-call | tf_op jit(solution)/shard_map/pallas_call | solution.py:426

commit v4 on v3

--- a/solution.py
+++ b/solution.py
@@ -42,9 +42,9 @@
     x_ref, gamma_ref, w1_ref, w2_ref, wo_ref, g_hbm,
     z_hbm, ag_hbm, wl_ref, wr_ref, dwo_ref, gain_ref,
     g_ref, xs, xh, nm, rs, wp, wpt, wf, rf, right_in, right, left, left_t, g_out, buf,
-    dl_out, dl_in, dr_out, dr_sib, dr_in, dl_own, dr_own,
+    dl_out, dl_in, dr_acc, dr_out, dr_sib, dr_in, dl_own, dr_own,
     dw_give, dw_sib, dw_own, dw_pair, dw_in, dw_blk, dw_chip, dw_full,
-    sm_give, sm_sib, sm_own, sm_col, sm_sum, sm_chip, sm_half, z_buf, ag_buf,
+    sm_give, sm_sib, sm_own, sm_out, sm_col, sm_sum, sm_chip, sm_half, z_buf, ag_buf,
     g_sem, z_sem, ag_sem, rg_s, rg_r, lg_s, lg_r, dl_s, dl_r, dr_s, dr_r,
     d1_s, d1_r, d2_s, d2_r, d3_s, d3_r, d4_s, d4_r, d5_s, d5_r,
     s1_s, s1_r, s2_s, s2_r, s3_s, s3_r, s4_s, s4_r,
@@ -170,31 +170,45 @@
 
     g_outer_part(n_go // 2, n_go)
 
+    HB = n_col // 2 * B
+    HI = I // 2
+
+    def turn_left(z, h):
+        for k in range(HB // S):
+            left_t[h, :, k * S:(k + 1) * S] = left[aligned(z * HB + k * S, S, S), :].T
+
+    def right_grad(z, h, p):
+        rhs = jnp.concatenate([
+            jnp.concatenate([
+                g_out[(2 * p + a) * C:(2 * p + a + 1) * C, aligned((z * HI + i) * J, J, J)]
+                for a in range(2)], axis=1)
+            for i in range(HI)], axis=0)
+        return mm(left_t[h], rhs)
+
+    for d in range(1, n_y):
+        wait_left(col_of(d, False))
+    turn_left(zl, 0)
+    for p in range(C // 2):
+        dr_acc[:, 2 * p * J:(2 * p + 2) * J] = right_grad(zl, 0, p)
+
     for d in range(1, n_x):
         block = row_of(d, False, False)
         wait_right(block)
         send_right(block, 2 * n_x + d, sib)
     for d in range(1, n_y):
-        wait_left(col_of(d, False))
-    for d in range(1, n_y):
         wait_left(col_of(d, True))
-    for d in range(1, n_x):
-        block = row_of(d, True, False)
-        wait_right(block)
-        send_right(block, 3 * n_x + d, sib)
-    for k in range(I * C // S):
-        left_t[:, k * S:(k + 1) * S] = left[k * S:(k + 1) * S, :].T
-
-    for h in range(C // 2):
-        rhs = jnp.concatenate([
-            jnp.concatenate([
-                g_out[(2 * h + a) * C:(2 * h + a + 1) * C, i * J:(i + 1) * J] for a in range(2)], axis=1)
-            for i in range(I)], axis=0)
-        acc = mm(left_t[...], rhs) * inv
+    turn_left(1 - zl, 1)
+    for p in range(C // 2):
+        if p == C // 8:
+            for d in range(1, n_x):
+                block = row_of(d, True, False)
+                wait_right(block)
+                send_right(block, 3 * n_x + d, sib)
+        acc = (dr_acc[:, 2 * p * J:(2 * p + 2) * J] + right_grad(1 - zl, 1, p)) * inv
         tiles = [acc[:, a * J:(a + 1) * J].T for a in range(2)]
         for q in range(n_row):
             blk = jnp.concatenate([t[q * T:(q + 1) * T] for t in tiles], axis=0)
-            dr_out[q % 2, q // 2, h * 2 * T:(h + 1) * 2 * T, :] = blk.astype(BF)
+            dr_out[q % 2, q // 2, p * 2 * T:(p + 1) * 2 * T, :] = blk.astype(BF)
     to_sib = remote(dr_out.at[1 - core], dr_sib, dr_s.at[0], dr_r.at[n_chip], row=sib)
     send(to_sib)
 
@@ -302,7 +316,7 @@
     RS = 2 * C
     for a in range(wide):
         sm_own[a, 0:RS, :] = wgrad[:, a * K:(a + 1) * K]
-        sm_own[a, RS:RS + 8, :] = jnp.broadcast_to(gain[:, a * K:(a + 1) * K], (8, K))
+        sm_own[a, RS:RS + 16, :] = jnp.broadcast_to(gain[:, a * K:(a + 1) * K], (16, K))
     sm_to_sib = remote(sm_own.at[1 - core], sm_sib, s1_s, s1_r, row=sib)
     send(sm_to_sib)
 
@@ -350,17 +364,25 @@
         c.start()
         z_copies.append(c)
 
+    def put_dw(h):
+        per = RW // C
+        for e in range(C // 2):
+            part = dw_full[h, e // per].astype(F32)
+            dwo_ref[pl.ds(h * (C // 2) + e, C, stride=C), :] = part[(e % per) * C:(e % per + 1) * C]
+
     z_part(0, 4)
     sm_to_sib.wait_recv()
     sm_give[...] = sm_own[core] + sm_sib[...]
-    to_cols(sm_give, sm_col, s2_s, s2_r)
+    sm_out[0] = sm_give[...].astype(BF)
+    to_cols(sm_out.at[0], sm_col, s2_s, s2_r)
     z_part(1, 4)
     own = dw_pair[col].astype(F32)
     dw_blk[0] = sum_cols(own, dw_in, d2_s, d2_r).astype(BF)
     to_chips(dw_blk.at[0], dw_chip, d3_s, d3_r)
     z_part(2, 4)
     sm_sum[...] = sum_cols(sm_give[...], sm_col, s2_s, s2_r)
-    to_chips(sm_sum, sm_chip, s3_s, s3_r)
+    sm_out[1] = sm_sum[...].astype(BF)
+    to_chips(sm_out.at[1], sm_chip, s3_s, s3_r)
     z_part(3, 4)
     dw_blk[1] = (sum_chips(dw_blk[0].astype(F32), dw_chip, d3_s, d3_r) * inv).astype(BF)
     to_cols(dw_blk.at[1], dw_full.at[core], d4_s, d4_r)
@@ -373,12 +395,7 @@
         got = dw_full.at[core, src]
         remote(got, got, d4_s.at[d], d4_r.at[src], col=src).wait_recv()
     send(remote(dw_full.at[core], dw_full.at[core], d5_s, d5_r.at[core], row=sib))
-
-    def put_dw(h):
-        per = RW // C
-        for e in range(C // 2):
-            part = dw_full[h, e // per].astype(F32)
-            dwo_ref[pl.ds(h * (C // 2) + e, C, stride=C), :] = part[(e % per) * C:(e % per + 1) * C]
+    put_dw(core)
 
     got = sm_half.at[1 - core]
     remote(got, got, s4_s, s4_r.at[1 - core], row=sib).wait_recv()
@@ -389,8 +406,7 @@
         gain_ref[:, lanes] = sm_half[a, RS:RS + 1, :]
     got = dw_full.at[1 - core]
     remote(got, got, d5_s, d5_r.at[1 - core], row=sib).wait_recv()
-    put_dw(0)
-    put_dw(1)
+    put_dw(1 - core)
 
     ag_copy.wait()
     for c in z_copies:
@@ -441,7 +457,7 @@
     B = T * C
     n_chip = n_row // 2
     RW = CC // 2 // n_col
-    RS = 2 * C + 8
+    RS = 2 * C + 16
     one = pltpu.SemaphoreType.DMA
     V = lambda shape, dtype: pltpu.VMEM(shape, dtype)
     D = lambda n: pltpu.SemaphoreType.DMA((n,))
@@ -472,11 +488,12 @@
             V((n_row, B, S), BF),
             V((C * J, S), BF),
             V((I * C, S), BF),
-            V((S, I * C), BF),
+            V((2, S, I * C // 2), BF),
             V((CC, I * J), BF),
             V((I * C, C * J), BF),
             V((n_col, B, S), BF),
             V((n_col, B, S), BF),
+            V((S, C * J), F32),
             V((2, n_chip, B, S), BF),
             V((n_chip, B, S), BF),
             V((n_chip, B, S), BF),
@@ -493,9 +510,10 @@
             V((RS, K), F32),
             V((RS, K), F32),
             V((2, RS, K), F32),
-            V((n_col, RS, K), F32),
+            V((2, RS, K), BF),
+            V((n_col, RS, K), BF),
             V((RS, K), F32),
-            V((n_chip, RS, K), F32),
+            V((n_chip, RS, K), BF),
             V((2, RS, K), F32),
             V((I * J, K), BF),
             V((S, T, M), BF),

time: 62 us -> 59.6 us (0.961)
  Pallas kernels: 61 us -> 58.7 us
    pallas_call x1, Pallas kernels: 58.1 us -> 55.8 us  [on_device(): pl.pallas_call(functools.partial(kernel, n_row, n_col), out_shape=(jax.Sh...]
where the time goes in v4:
time: 59.6 us; the launch traced here: 59.5 us
  Pallas kernels  58.7 us (98%)
  between operations  0.82 us (1%)
    pallas_call x1, Pallas kernels, on_device(): pl.pallas_call(functools.partial(kernel, n_row, n_col), out_shape=(jax.Sh...  55.8 us
    pallas_call x1, Pallas kernels, settle(): pl.pallas_call(settle_kernel, out_shape=tuple((jax.ShapeDtypeStruct(a.sha...  2.88 us

profile of v4, /device:TPU:1, one launch (start us, length us, event | category | flops | bytes accessed | tf_op | source)
XLA Modules:
  0.0 59.5 jit_solution(15405810397474164836)
XLA Ops:
  0.6 55.8 %shard_map.109 = (bf16[8192,128]{1,0:T(8,128)(2,1)}, bf16[128,8,256]{2,1,0:T(8,128)(2,1)}, f32[32,256]{1,0:T(8,128)}, f32[32,256]{1,0:T(8,128)}, f32[1024,128]{1,0:T(8,128)}, /*index=5*/f32[1,256]{1,0:T(1,128)}) custom-call(bf16[128,8,256]{2,1,0:T(8,128)(2,1)} %x_ref.1, f32[1,256]{1,0:T(1,128)} %bitcast.11, bf16[32,256]{1,0:T(8,128)(2,1)} %bitcast.9, ...), custom_call_target="tpu_custom_call" | custom-call | tf_op jit(solution)/shard_map/pallas_call | solution.py:466
  56.4 2.9 %shard_map.110 = (bf16[8192,128]{1,0:T(8,128)(2,1)}, bf16[128,8,256]{2,1,0:T(8,128)(2,1)}, f32[32,256]{1,0:T(8,128)}, f32[32,256]{1,0:T(8,128)}, f32[1024,128]{1,0:T(8,128)}, /*index=5*/f32[1,256]{1,0:T(1,128)}) custom-call(bf16[8192,128]{1,0:T(8,128)(2,1)} %get-tuple-element.18.refs_0_, bf16[128,8,256]{2,1,0:T(8,128)(2,1)} %get-tuple-element.19.refs_1_, ...), custom_call_target="tpu_custom_call" | custom-call | tf_op jit(solution)/shard_map/pallas_call | solution.py:442

commit v5 on v4

--- a/solution.py
+++ b/solution.py
@@ -39,14 +39,15 @@
 
 def kernel(
     n_row, n_col,
-    x_ref, gamma_ref, w1_ref, w2_ref, wo_ref, g_hbm,
-    z_hbm, ag_hbm, wl_ref, wr_ref, dwo_ref, gain_ref,
+    x_hbm, gamma_hbm, w1_hbm, w2_hbm, wo_hbm, g_hbm,
+    z_hbm, ag_hbm, wl_hbm, wr_hbm, dwo_hbm, gain_hbm,
+    x_ref, gamma_ref, w1_ref, w2_ref, wo_ref,
     g_ref, xs, xh, nm, rs, wp, wpt, wf, rf, right_in, right, left, left_t, g_out, buf,
     dl_out, dl_in, dr_acc, dr_out, dr_sib, dr_in, dl_own, dr_own,
     dw_give, dw_sib, dw_own, dw_pair, dw_in, dw_blk, dw_chip, dw_full,
-    sm_give, sm_sib, sm_own, sm_out, sm_col, sm_sum, sm_chip, sm_half, z_buf, ag_buf,
-    g_sem, z_sem, ag_sem, rg_s, rg_r, lg_s, lg_r, dl_s, dl_r, dr_s, dr_r,
-    d1_s, d1_r, d2_s, d2_r, d3_s, d3_r, d4_s, d4_r, d5_s, d5_r,
+    sm_give, sm_sib, sm_own, sm_out, sm_col, sm_sum, sm_chip, sm_half, z_buf, ag_buf, wl, wr, dwo, gain_buf,
+    in_sem, g_sem, z_sem, ag_sem, out_sem, rg_s, rg_r, lg_s, lg_r, dl_s, dl_r, dr_s, dr_r,
+    d1_s, d1_r, d2_s, d2_r, d3_s, d3_r, d4_s, d4_r,
     s1_s, s1_r, s2_s, s2_r, s3_s, s3_r, s4_s, s4_r,
 ):
     S, T, M = x_ref.shape
@@ -92,9 +93,20 @@
         pl.semaphore_signal(barrier, inc=1, device_id={"row": peer}, device_id_type=MESH)
     for d in range(1, n_col):
         pl.semaphore_signal(barrier, inc=1, device_id={"col": other_col(d)}, device_id_type=MESH)
-
+        pl.semaphore_signal(
+            barrier, inc=1, device_id={"row": sib, "col": other_col(d)}, device_id_type=MESH)
+
+    loads = [
+        pltpu.make_async_copy(src, dst, in_sem.at[k])
+        for k, (src, dst) in enumerate((
+            (x_hbm, x_ref), (gamma_hbm, gamma_ref), (w1_hbm, w1_ref), (w2_hbm, w2_ref), (wo_hbm, wo_ref)))
+    ]
+    for c in loads:
+        c.start()
     g_copy = pltpu.make_async_copy(g_hbm, g_ref, g_sem)
     g_copy.start()
+    for c in loads[:4]:
+        c.wait()
 
     wcat = jnp.concatenate([w1_ref[...], w2_ref[...]], axis=0)
     gamma = gamma_ref[...]
@@ -116,7 +128,7 @@
         rf[pl.ds(t, C, stride=T), :] = proj[C:]
     right_in[row] = rf[...].astype(BF)
 
-    pl.semaphore_wait(barrier, n_chip + n_col - 1)
+    pl.semaphore_wait(barrier, n_chip + 2 * (n_col - 1))
 
     def left_rows(c):
         return aligned(c * B, B, B)
@@ -143,6 +155,7 @@
         send_left(col, d, col_of(d, False))
     send_right(row, 2 * n_x, sib)
 
+    loads[4].wait()
     wf[...] = wo_ref[...].astype(F32)
     for e in range(C):
         wp[e * C:(e + 1) * C, :] = wf[pl.ds(e, C, stride=C), :].astype(BF)
@@ -364,12 +377,6 @@
         c.start()
         z_copies.append(c)
 
-    def put_dw(h):
-        per = RW // C
-        for e in range(C // 2):
-            part = dw_full[h, e // per].astype(F32)
-            dwo_ref[pl.ds(h * (C // 2) + e, C, stride=C), :] = part[(e % per) * C:(e % per + 1) * C]
-
     z_part(0, 4)
     sm_to_sib.wait_recv()
     sm_give[...] = sm_own[core] + sm_sib[...]
@@ -385,28 +392,54 @@
     to_chips(sm_out.at[1], sm_chip, s3_s, s3_r)
     z_part(3, 4)
     dw_blk[1] = (sum_chips(dw_blk[0].astype(F32), dw_chip, d3_s, d3_r) * inv).astype(BF)
-    to_cols(dw_blk.at[1], dw_full.at[core], d4_s, d4_r)
+    def give_dw(slot, **where):
+        send(remote(dw_blk.at[1], dw_full.at[core, col], d4_s.at[slot], d4_r.at[core, col], **where))
+
+    for d in range(1, n_col):
+        give_dw(d, col=other_col(d))
+        give_dw(n_col + d, row=sib, col=other_col(d))
+    give_dw(0, row=sib)
     dw_full[core, col] = dw_blk[1]
     sm_half[core] = sum_chips(sm_sum[...], sm_chip, s3_s, s3_r)
     sm_back = remote(sm_half.at[core], sm_half.at[core], s4_s, s4_r.at[core], row=sib)
     send(sm_back)
+    def wait_dw(h, src):
+        got = dw_full.at[h, src]
+        remote(got, got, d4_s.at[0], d4_r.at[h, src], row=sib).wait_recv()
+
     for d in range(1, n_col):
-        src = lax.rem(col + n_col - d, n_col)
-        got = dw_full.at[core, src]
-        remote(got, got, d4_s.at[d], d4_r.at[src], col=src).wait_recv()
-    send(remote(dw_full.at[core], dw_full.at[core], d5_s, d5_r.at[core], row=sib))
+        wait_dw(core, lax.rem(col + n_col - d, n_col))
+
+    def put_dw(h):
+        per = RW // C
+        for e in range(C // 2):
+            part = dw_full[h, e // per, (e % per) * C:(e % per + 1) * C, :]
+            dwo[pl.ds(h * (C // 2) + e, C, stride=C), :] = part.astype(F32)
+
     put_dw(core)
 
     got = sm_half.at[1 - core]
     remote(got, got, s4_s, s4_r.at[1 - core], row=sib).wait_recv()
     for a in range(wide):
         lanes = slice(a * K, (a + 1) * K)
-        wl_ref[:, lanes] = sm_half[a, 0:C, :]
-        wr_ref[:, lanes] = sm_half[a, C:2 * C, :]
-        gain_ref[:, lanes] = sm_half[a, RS:RS + 1, :]
-    got = dw_full.at[1 - core]
-    remote(got, got, d5_s, d5_r.at[1 - core], row=sib).wait_recv()
+        wl[:, lanes] = sm_half[a, 0:C, :]
+        wr[:, lanes] = sm_half[a, C:2 * C, :]
+        gain_buf[:, lanes] = sm_half[a, RS:RS + 1, :]
+    outs = []
+
+    def put(src, dst):
+        outs.append(pltpu.make_async_copy(src, dst, out_sem.at[len(outs)]))
+        outs[-1].start()
+
+    put(wl, wl_hbm)
+    put(wr, wr_hbm)
+    put(gain_buf, gain_hbm)
+    for d in range(n_col):
+        wait_dw(1 - core, lax.rem(col + n_col - d, n_col))
     put_dw(1 - core)
+    put(dwo, dwo_hbm)
+    for c in outs:
+        c.wait()
 
     ag_copy.wait()
     for c in z_copies:
@@ -461,9 +494,8 @@
     one = pltpu.SemaphoreType.DMA
     V = lambda shape, dtype: pltpu.VMEM(shape, dtype)
     D = lambda n: pltpu.SemaphoreType.DMA((n,))
-    vm = pl.BlockSpec(memory_space=pltpu.VMEM)
     hb = pl.BlockSpec(memory_space=pl.ANY)
-    z, ag, wl, wr, dwo, gain = pl.pallas_call(
+    parts = pl.pallas_call(
         functools.partial(kernel, n_row, n_col),
         out_shape=(
             jax.ShapeDtypeStruct((I * J, K), BF),
@@ -473,9 +505,14 @@
             jax.ShapeDtypeStruct((CC, K), F32),
             jax.ShapeDtypeStruct((1, M), F32),
         ),
-        in_specs=[vm, vm, vm, vm, vm, hb],
-        out_specs=(hb, hb, vm, vm, vm, vm),
+        in_specs=[hb] * 6,
+        out_specs=(hb,) * 6,
         scratch_shapes=[
+            V((S, T, M), BF),
+            V((1, M), F32),
+            V((C, M), BF),
+            V((C, M), BF),
+            V((CC, K), BF),
             V((I * J, K), BF),
             V((M // K, S * T, K), F32),
             V((T, S, M), F32),
@@ -517,16 +554,20 @@
             V((2, RS, K), F32),
             V((I * J, K), BF),
             V((S, T, M), BF),
-            one, D(4), one,
+            V((C, M), F32),
+            V((C, M), F32),
+            V((CC, K), F32),
+            V((1, M), F32),
+            D(5), one, D(4), one, D(4),
             D(n_row), D(n_row), D(n_col), D(n_col), D(n_col), D(n_col), D(n_chip), D(n_chip + 1),
-            one, one, D(n_col), D(n_col), D(n_chip), D(n_chip), D(n_col), D(n_col), one, D(2),
+            one, one, D(n_col), D(n_col), D(n_chip), D(n_chip), D(2 * n_col), pltpu.SemaphoreType.DMA((2, n_col)),
             one, one, D(n_col), D(n_col), D(n_chip), D(n_chip), one, D(2),
         ],
         compiler_params=pltpu.CompilerParams(
             collective_id=0, has_side_effects=True, vmem_limit_bytes=56 * 1024 * 1024,
         ),
     )(x, gamma.reshape(1, M), w1.T, w2.T, wo, cot.reshape(I * J, K))
-    z, ag, wl, wr, dwo, gain = settle((z, ag, wl, wr, dwo, gain))
+    z, ag, wl, wr, dwo, gain = settle(parts)
     return z.reshape(cot.shape), ag, wl.T, wr.T, dwo, gain.reshape(M)
 
 

time: 59.6 us -> 58.7 us (0.985)
  Pallas kernels: 58.7 us -> 57.8 us
    pallas_call x1, Pallas kernels: 55.8 us -> 54.9 us  [on_device(): pl.pallas_call(functools.partial(kernel, n_row, n_col), out_shape=(jax.Sh...]
where the time goes in v5:
time: 58.7 us; the launch traced here: 58.6 us
  Pallas kernels  57.8 us (98%)
  between operations  0.82 us (1%)
    pallas_call x1, Pallas kernels, on_device(): pl.pallas_call(functools.partial(kernel, n_row, n_col), out_shape=(jax.Sh...  54.9 us
    pallas_call x1, Pallas kernels, settle(): pl.pallas_call(settle_kernel, out_shape=tuple((jax.ShapeDtypeStruct(a.sha...  2.88 us

profile of v5, /device:TPU:1, one launch (start us, length us, event | category | flops | bytes accessed | tf_op | source)
XLA Modules:
  0.0 58.6 jit_solution(3710269307139939649)
XLA Ops:
  0.6 54.9 %shard_map.109 = (bf16[8192,128]{1,0:T(8,128)(2,1)}, bf16[128,8,256]{2,1,0:T(8,128)(2,1)}, f32[32,256]{1,0:T(8,128)}, f32[32,256]{1,0:T(8,128)}, f32[1024,128]{1,0:T(8,128)}, /*index=5*/f32[1,256]{1,0:T(1,128)}) custom-call(bf16[128,8,256]{2,1,0:T(8,128)(2,1)} %x_hbm.1, f32[1,256]{1,0:T(1,128)} %bitcast.11, bf16[32,256]{1,0:T(8,128)(2,1)} %bitcast.9, ...), custom_call_target="tpu_custom_call" | custom-call | tf_op jit(solution)/shard_map/pallas_call | solution.py:498
  55.5 2.9 %shard_map.110 = (bf16[8192,128]{1,0:T(8,128)(2,1)}, bf16[128,8,256]{2,1,0:T(8,128)(2,1)}, f32[32,256]{1,0:T(8,128)}, f32[32,256]{1,0:T(8,128)}, f32[1024,128]{1,0:T(8,128)}, /*index=5*/f32[1,256]{1,0:T(1,128)}) custom-call(bf16[8192,128]{1,0:T(8,128)(2,1)} %get-tuple-element.18.refs_0_, bf16[128,8,256]{2,1,0:T(8,128)(2,1)} %get-tuple-element.19.refs_1_, ...), custom_call_target="tpu_custom_call" | custom-call | tf_op jit(solution)/shard_map/pallas_call | solution.py:475

commit v6 on v5

--- a/solution.py
+++ b/solution.py
@@ -212,7 +212,7 @@
         wait_left(col_of(d, True))
     turn_left(1 - zl, 1)
     for p in range(C // 2):
-        if p == C // 8:
+        if p == 0:
             for d in range(1, n_x):
                 block = row_of(d, True, False)
                 wait_right(block)

time: 58.7 us -> 58.6 us (level)
  no operation moved by 1% of the time
where the time goes in v6:
time: 58.6 us; the launch traced here: 58.5 us
  Pallas kernels  57.7 us (98%)
  between operations  0.82 us (1%)
    pallas_call x1, Pallas kernels, on_device(): pl.pallas_call(functools.partial(kernel, n_row, n_col), out_shape=(jax.Sh...  54.8 us
    pallas_call x1, Pallas kernels, settle(): pl.pallas_call(settle_kernel, out_shape=tuple((jax.ShapeDtypeStruct(a.sha...  2.88 us

profile of v6, /device:TPU:1, one launch (start us, length us, event | category | flops | bytes accessed | tf_op | source)
XLA Modules:
  0.0 58.5 jit_solution(16997583155628872625)
XLA Ops:
  0.6 54.8 %shard_map.109 = (bf16[8192,128]{1,0:T(8,128)(2,1)}, bf16[128,8,256]{2,1,0:T(8,128)(2,1)}, f32[32,256]{1,0:T(8,128)}, f32[32,256]{1,0:T(8,128)}, f32[1024,128]{1,0:T(8,128)}, /*index=5*/f32[1,256]{1,0:T(1,128)}) custom-call(bf16[128,8,256]{2,1,0:T(8,128)(2,1)} %x_hbm.1, f32[1,256]{1,0:T(1,128)} %bitcast.11, bf16[32,256]{1,0:T(8,128)(2,1)} %bitcast.9, ...), custom_call_target="tpu_custom_call" | custom-call | tf_op jit(solution)/shard_map/pallas_call | solution.py:498
  55.4 2.9 %shard_map.110 = (bf16[8192,128]{1,0:T(8,128)(2,1)}, bf16[128,8,256]{2,1,0:T(8,128)(2,1)}, f32[32,256]{1,0:T(8,128)}, f32[32,256]{1,0:T(8,128)}, f32[1024,128]{1,0:T(8,128)}, /*index=5*/f32[1,256]{1,0:T(1,128)}) custom-call(bf16[8192,128]{1,0:T(8,128)(2,1)} %get-tuple-element.18.refs_0_, bf16[128,8,256]{2,1,0:T(8,128)(2,1)} %get-tuple-element.19.refs_1_, ...), custom_call_target="tpu_custom_call" | custom-call | tf_op jit(solution)/shard_map/pallas_call | solution.py:475
